TPU v7x, 32 devices: a whole 2x2x4 slice. The times are simulated.
32 devices in a mesh: dp: 2 (over x), ep: 16 (over z, y, core).
Axes of the slice: x: 2, y: 2, z: 4, core: 2. Of those that a mesh axis runs over, the one named last changes fastest.
Arguments:
- tokens: bfloat16 [4096, 2048], P(('dp', 'ep'))
- cotangent: bfloat16 [4096, 2048], P(('dp', 'ep'))
- expert_ids: int32 [4096, 8], P(('dp', 'ep')), may hold values from 0 to 15, all different within a row; in each aligned block of 128 rows (0 to 127, 128 to 255, ...) at most 72 rows name the same one
- route_weights: bfloat16 [4096, 8], P(('dp', 'ep')), may hold values from 0.029907227 to 0.3984375
- weights: bfloat16 [16, 3, 2048, 384], P('ep')
- first_moment: bfloat16 [16, 3, 2048, 384], P('ep', None, 'dp'), may hold values from -4 to 4
- second_moment: bfloat16 [16, 3, 2048, 384], P('ep', None, 'dp'), may hold values from 0.049804688 to 0.5
Outputs:
- token_grad: bfloat16 [4096, 2048], P(('dp', 'ep'))
- routing_grad: bfloat16 [4096, 8], P(('dp', 'ep'))
- new_first: bfloat16 [16, 3, 2048, 384], P('ep', None, 'dp')
- new_second: bfloat16 [16, 3, 2048, 384], P('ep', None, 'dp')
- update: bfloat16 [16, 3, 2048, 384], P('ep', None, 'dp')
Inputs may be any that keep to these rules, and one draw needn't show every extreme that they name: `expert_ids`: among the 128 rows of one device no expert is named by more than 72 rows.
All inputs are finite; a program needn't handle non-finite values.
Results may differ from a plain program's by a relative error of at most 0.0057.
Values may be sent and summed in bfloat16 or wider, within the bound.
A program may use at most 128 MiB of HBM per device.

v0:
```python
import jax
import jax.numpy as jnp
from jax import lax
from jax.sharding import PartitionSpec as P

ADAM_STEP = 10


def on_device(tokens, cotangent, expert_ids, route_weights, weights, first_moment, second_moment):
    tok_count, model_width = tokens.shape
    topk_count = expert_ids.shape[1]
    local_experts = weights.shape[0]
    hidden_units = weights.shape[3]
    groups = lax.axis_size("ep")
    experts = local_experts * groups
    capacity = (tok_count * topk_count * 9 + 8 * experts - 1) // (8 * experts)
    pairs = tok_count * topk_count
    ids_flat = expert_ids.reshape(-1)
    onehot = (ids_flat[:, None] == jnp.arange(experts, dtype=jnp.int32)[None, :]).astype(jnp.int32)
    position = jnp.sum(jnp.cumsum(onehot, 0) * onehot, 1) - 1
    target = ids_flat * capacity + position
    token_row = jnp.arange(pairs, dtype=jnp.int32) // topk_count
    send_tokens = (
        jnp.zeros((experts * capacity, model_width), jnp.bfloat16).at[target].set(tokens[token_row])
    )
    send_cot = (
        jnp.zeros((experts * capacity, model_width), jnp.bfloat16)
        .at[target]
        .set(cotangent[token_row])
    )
    send_weight = (
        jnp.zeros((experts * capacity,), jnp.bfloat16).at[target].set(route_weights.reshape(-1))
    )
    send_tokens = send_tokens.reshape(experts, capacity, model_width)
    send_cot = send_cot.reshape(experts, capacity, model_width)
    send_weight = send_weight.reshape(experts, capacity)
    recv_x, recv_cot, recv_weight = (
        lax.all_to_all(send_tokens, "ep", split_axis=0, concat_axis=1, tiled=True),
        lax.all_to_all(send_cot, "ep", split_axis=0, concat_axis=1, tiled=True),
        lax.all_to_all(send_weight, "ep", split_axis=0, concat_axis=1, tiled=True),
    )
    w_gate = weights[:, 0]
    w_up = weights[:, 1]
    w_down = weights[:, 2]
    gate_val = jnp.einsum("erd,edh->erh", recv_x, w_gate, preferred_element_type=jnp.float32)
    up_val = jnp.einsum("erd,edh->erh", recv_x, w_up, preferred_element_type=jnp.float32)
    sigmoid_gate = jax.nn.sigmoid(gate_val)
    activated = gate_val * sigmoid_gate
    hidden = lax.optimization_barrier((activated * up_val).astype(jnp.bfloat16))
    back_val = jnp.einsum("erd,edh->erh", recv_cot, w_down, preferred_element_type=jnp.float32)
    route_part = lax.optimization_barrier(
        jnp.sum(hidden.astype(jnp.float32) * back_val, 2).astype(jnp.bfloat16)
    )
    row_weight = recv_weight.astype(jnp.float32)[:, :, None]
    scaled = row_weight * back_val
    dgate = (scaled * up_val * sigmoid_gate * (1.0 + gate_val * (1.0 - sigmoid_gate))).astype(
        jnp.bfloat16
    )
    dup = (scaled * activated).astype(jnp.bfloat16)
    down_cot = (row_weight * recv_cot.astype(jnp.float32)).astype(jnp.bfloat16)
    slot_back = jnp.einsum("erh,edh->erd", dgate, w_gate, preferred_element_type=jnp.float32)
    slot_back = slot_back + jnp.einsum(
        "erh,edh->erd", dup, w_up, preferred_element_type=jnp.float32
    )
    slot_back = lax.optimization_barrier(slot_back.astype(jnp.bfloat16))
    ret_rows, ret_route = (
        lax.all_to_all(slot_back, "ep", split_axis=1, concat_axis=0, tiled=True),
        lax.all_to_all(route_part, "ep", split_axis=1, concat_axis=0, tiled=True),
    )
    picked = ret_rows.reshape(experts * capacity, model_width)[target]
    token_grad = jnp.sum(
        picked.reshape(tok_count, topk_count, model_width).astype(jnp.float32), 1
    ).astype(jnp.bfloat16)
    routing_grad = ret_route.reshape(-1)[target].reshape(tok_count, topk_count)
    grad_local = jnp.stack(
        [
            jnp.einsum("erd,erh->edh", recv_x, dgate, preferred_element_type=jnp.float32),
            jnp.einsum("erd,erh->edh", recv_x, dup, preferred_element_type=jnp.float32),
            jnp.einsum("erd,erh->edh", down_cot, hidden, preferred_element_type=jnp.float32),
        ],
        1,
    )
    grad_share = lax.psum_scatter(grad_local, "dp", scatter_dimension=2, tiled=True)
    square_sum = lax.psum(jnp.sum(grad_share * grad_share), ("dp", "ep"))
    param_count = 3.0 * experts * model_width * hidden_units
    root_mean = jnp.sqrt(square_sum / param_count + 1e-06)
    clip_factor = jnp.minimum(1.0, 0.5 / root_mean)
    clipped = clip_factor * grad_share
    first_next = 0.9 * first_moment.astype(jnp.float32) + 0.1 * clipped
    second_next = 0.95 * second_moment.astype(jnp.float32) + 0.05 * clipped * clipped
    update = (
        first_next
        / (1.0 - 0.9**ADAM_STEP)
        / (jnp.sqrt(second_next / (1.0 - 0.95**ADAM_STEP)) + 1e-08)
    )
    return (
        token_grad,
        routing_grad,
        first_next.astype(jnp.bfloat16),
        second_next.astype(jnp.bfloat16),
        update.astype(jnp.bfloat16),
    )


def solution(mesh):
    in_specs = (
        P(("dp", "ep"), None),
        P(("dp", "ep"), None),
        P(("dp", "ep"), None),
        P(("dp", "ep"), None),
        P("ep", None, None, None),
        P("ep", None, "dp", None),
        P("ep", None, "dp", None),
    )
    out_specs = (
        P(("dp", "ep"), None),
        P(("dp", "ep"), None),
        P("ep", None, "dp", None),
        P("ep", None, "dp", None),
        P("ep", None, "dp", None),
    )
    return jax.shard_map(
        on_device, mesh=mesh, in_specs=in_specs, out_specs=out_specs, check_vma=False
    )
```

profile of v0, /device:TPU:0, one launch (start us, length us, event | category | flops | bytes accessed | tf_op | source)
XLA Modules:
  0.0 598.7 jit_solution(5677673734785645098)
XLA Ops:
  7.2 0.7 broadcast_multiply_fusion
  7.9 0.8 copy.46
  8.7 0.1 eq.29
  8.8 0.1 eq.25
  8.9 0.8 copy.50
  9.7 0.1 reshape.350
  9.8 0.1 copy.45
  9.9 0.1 mul.121
  10.0 4.5 reduce-window.6
  14.6 0.1 copy.48
  15.0 7.6 %scatter_custom_fusion = bf16[1152]{0:T(1024)(128)(2,1)S(1)} fusion(s32[1024]{0:T(1024)S(1)} %bitcast.88, bf16[1024]{0:T(1024)(128)(2,1)S(1)} %reshape.350, bf16[]{:T(256)} %constant.21.clone.1), kind=kCustom, calls=%fused_computation.75 | custom fusion | bytes 2306 | tf_op jit(solution)/shard_map/scatter | solution.py:32
  22.6 0.7 all_to_all.23
  23.3 7.6 %all-to-all-start = ((bf16[16,1,72]{2,1,0:T(2,128)(2,1)}), bf16[16,1,72]{2,1,0:T(2,128)(2,1)S(1)}, u32[]{:S(2)}, u32[]{:S(2)}) async-start(bf16[16,1,72]{2,1,0:T(2,128)(2,1)} %all_to_all.23), calls=%async_computation | async-start | bytes 16384 | tf_op jit(solution)/shard_map/all_to_all | solution.py:40
  31.0 23.3 %scatter_custom_fusion.2 = bf16[1152,2048]{1,0:T(8,128)(2,1)} fusion(s32[1024]{0:T(1024)S(1)} %bitcast.89, bf16[128,2048]{1,0:T(8,128)(2,1)S(1)} %copy-done, s32[1024]{0:T(1024)S(1)} %broadcast_clamp_fusion.1, bf16[]{:T(256)} %constant.21.clone.1), kind=kCustom, calls=%fused_computation.23 | custom fusion | bytes 4718594 | tf_op jit(solution)/shard_map/scatter | solution.py:24
  54.3 6.2 %all-to-all-start.2 = ((bf16[16,72,2048]{2,1,0:T(8,128)(2,1)}), bf16[16,72,2048]{2,1,0:T(8,128)(2,1)}, u32[]{:S(2)}, u32[]{:S(2)}) async-start(bf16[16,72,2048]{2,1,0:T(8,128)(2,1)} %bitcast.85), calls=%async_computation.2 | async-start | bytes 9437184 | tf_op jit(solution)/shard_map/all_to_all | solution.py:38
  60.4 23.4 %scatter_custom_fusion.1 = bf16[1152,2048]{1,0:T(8,128)(2,1)} fusion(s32[1024]{0:T(1024)S(1)} %bitcast.90, bf16[128,2048]{1,0:T(8,128)(2,1)} %param.8, s32[1024]{0:T(1024)S(1)} %broadcast_clamp_fusion.1, bf16[]{:T(256)} %constant.21.clone.1), kind=kCustom, calls=%fused_computation.25 | custom fusion | bytes 4719104 | tf_op jit(solution)/shard_map/scatter | solution.py:29
  83.8 63.4 %all-to-all-done.2 = bf16[16,72,2048]{2,1,0:T(8,128)(2,1)} async-done(((bf16[16,72,2048]{2,1,0:T(8,128)(2,1)}), bf16[16,72,2048]{2,1,0:T(8,128)(2,1)}, u32[]{:S(2)}, u32[]{:S(2)}) %all-to-all-start.2) | async-done | bytes 4718624 | tf_op jit(solution)/shard_map/all_to_all | solution.py:38
  147.3 21.8 %all-to-all-start.1 = ((bf16[16,72,2048]{2,1,0:T(8,128)(2,1)}), bf16[16,72,2048]{2,1,0:T(8,128)(2,1)}, u32[]{:S(2)}, u32[]{:S(2)}) async-start(bf16[16,72,2048]{2,1,0:T(8,128)(2,1)} %bitcast.84), calls=%async_computation.1 | async-start | bytes 9437184 | tf_op jit(solution)/shard_map/all_to_all | solution.py:39
  169.2 6.3 %fusion.23 = f32[1152,384]{0,1:T(8,128)} fusion(bf16[1152,2048]{1,0:T(8,128)(2,1)} %bitcast.9, bf16[1,3,2048,384]{3,2,1,0:T(8,128)(2,1)} %param.11), kind=kOutput, calls=%fused_computation.43 | convolution fusion | flops 1811939328 | bytes 8060928 | tf_op jit(solution)/shard_map/erd,edh->erh/dot_general | solution.py:45
  175.5 80.3 %all-to-all-done.1 = bf16[16,72,2048]{2,1,0:T(8,128)(2,1)} async-done(((bf16[16,72,2048]{2,1,0:T(8,128)(2,1)}), bf16[16,72,2048]{2,1,0:T(8,128)(2,1)}, u32[]{:S(2)}, u32[]{:S(2)}) %all-to-all-start.1) | async-done | bytes 4718624 | tf_op jit(solution)/shard_map/all_to_all | solution.py:39
  255.9 5.2 fusion.28
  261.1 5.8 multiply_convert_fusion.1
  266.9 5.4 convolution_bitcast_fusion
  272.3 4.7 convolution_bitcast_fusion.1
  277.1 5.3 fusion.12
  282.4 4.2 pad_maximum_fusion
  286.7 1.4 fusion.19
  288.1 0.7 all_to_all.24
  288.8 22.0 %all-to-all-start.4 = ((bf16[1,16,72]{2,0,1:T(2,128)(2,1)}), bf16[1,16,72]{2,0,1:T(2,128)(2,1)S(1)}, u32[]{:S(2)}, u32[]{:S(2)}) async-start(bf16[1,16,72]{2,0,1:T(2,128)(2,1)} %all_to_all.24), calls=%async_computation.4 | async-start | bytes 16384 | tf_op jit(solution)/shard_map/all_to_all | solution.py:68
  310.8 4.2 fusion.21
  314.9 4.1 fusion.2
  319.0 27.6 %copy.68 = bf16[1,1152,2048]{2,0,1:T(2,128)(2,1)} copy(bf16[1,1152,2048]{2,1,0:T(8,128)(2,1)S(1)} %fusion.2) | data formatting | bytes 9437184 | tf_op jit(solution)/shard_map/optimization_barrier | solution.py:65
  346.6 0.5 broadcast.194
  347.2 29.9 %reduce.8 = bf16[1152,2048]{1,0:T(8,128)(2,1)} reduce(bf16[1152,1,2048]{2,1,0:T(2,128)(2,1)} %bitcast.82, bf16[]{:T(256)} %broadcast.194), dimensions={1}, to_apply=%bitcast.77.reduce_sub_computation | reduce | bytes 9437186
  377.0 13.3 %reshape.393 = bf16[16,2,73728]{2,1,0:T(2,128)(2,1)} reshape(bf16[1152,2048]{1,0:T(8,128)(2,1)} %reduce.8) | data formatting | bytes 9437184
  390.3 6.4 %all-to-all-start.3 = ((bf16[16,2,73728]{2,1,0:T(2,128)(2,1)}), bf16[16,2,73728]{2,1,0:T(2,128)(2,1)}, u32[]{:S(2)}, u32[]{:S(2)}) async-start(bf16[16,2,73728]{2,1,0:T(2,128)(2,1)} %reshape.393), calls=%async_computation.3 | async-start | bytes 9437184 | tf_op jit(solution)/shard_map/all_to_all | solution.py:67
  396.8 0.1 reshape.309
  396.9 6.8 %gather_fusion.1 = bf16[1024]{0:T(1024)(128)(2,1)S(1)} fusion(bf16[1152]{0:T(1024)(128)(2,1)S(1)} %reshape.309, s32[1024]{0:T(1024)S(1)} %broadcast_clamp_fusion), kind=kCustom, calls=%fused_computation.3 | custom fusion | bytes 8192 | tf_op jit(solution)/shard_map/gather | solution.py:74
  403.7 0.1 reshape.310
  403.8 0.7 copy.59
  404.5 79.1 %all-to-all-done.3 = bf16[16,2,73728]{2,1,0:T(2,128)(2,1)} async-done(((bf16[16,2,73728]{2,1,0:T(2,128)(2,1)}), bf16[16,2,73728]{2,1,0:T(2,128)(2,1)}, u32[]{:S(2)}, u32[]{:S(2)}) %all-to-all-start.3) | async-done | bytes 4718624 | tf_op jit(solution)/shard_map/all_to_all | solution.py:67
  483.6 12.8 %reshape.394 = bf16[1152,1,2048]{2,1,0:T(2,128)(2,1)} reshape(bf16[16,2,73728]{2,1,0:T(2,128)(2,1)} %all-to-all-done.3) | data formatting | bytes 9437184
  496.4 8.9 %copy.67 = bf16[1,1152,2048]{2,1,0:T(8,128)(2,1)} copy(bf16[1,1152,2048]{2,0,1:T(2,128)(2,1)} %bitcast.83) | data formatting | bytes 9437184
  505.3 11.8 %gather_fusion = bf16[1024,2048]{1,0:T(8,128)(2,1)} fusion(bf16[1152,2048]{1,0:T(8,128)(2,1)} %bitcast.81, s32[1024]{0:T(1024)S(1)} %broadcast_clamp_fusion), kind=kCustom, calls=%fused_computation.2 | custom fusion | bytes 8392704 | tf_op jit(solution)/shard_map/gather | solution.py:70
  517.1 4.3 multiply_reduce_fusion
  521.4 3.7 bitcast_reduce_fusion
  525.1 57.8 %psum.7 = f32[]{:T(128)} all-reduce(f32[]{:T(128)} %multiply_reduce_fusion), channel_id=1, replica_groups=mesh['dp'=2,'ep'=16] {'dp','ep'}, use_global_device_ids=true, to_apply=%region_10.11 | all-reduce | flops 1 | bytes 8 | tf_op jit(solution)/shard_map/psum | solution.py:84
  583.6 7.8 %divide_convert_fusion = (bf16[1,3,1024,384]{3,2,1,0:T(8,128)(2,1)}, bf16[1,3,1024,384]{3,2,1,0:T(8,128)(2,1)}, bf16[1,3,1024,384]{3,2,1,0:T(8,128)(2,1)}) fusion(f32[1,3,1024,384]{3,2,1,0:T(8,128)} %reduce-scatter.2.cloned.1.call-done, bf16[1,3,1024,384]{3,2,1,0:T(8,128)(2,1)S(1)} %copy-done.3, bf16[1,3,1024,384]{3,2,1,0:T(8,128)(2,1)} %param.13, f32[]{:T(128)S(6)} %min.3), kind=kLoop, calls=%fused_computation.18 | loop fusion | flops 20054016 | bytes 16515076 | tf_op jit(solution)/shard_map/convert_element_type | solution.py:101
  (38 shorter events, 0.6 us)
Async XLA Ops:
  7.2 23.8 %copy-start = (bf16[128,2048]{1,0:T(8,128)(2,1)S(1)}, bf16[128,2048]{1,0:T(8,128)(2,1)}, u32[]{:S(2)}) copy-start(bf16[128,2048]{1,0:T(8,128)(2,1)} %param.7) | copy-start | bytes 1572868
  23.3 31.0 %all-to-all-start = ((bf16[16,1,72]{2,1,0:T(2,128)(2,1)}), bf16[16,1,72]{2,1,0:T(2,128)(2,1)S(1)}, u32[]{:S(2)}, u32[]{:S(2)}) async-start(bf16[16,1,72]{2,1,0:T(2,128)(2,1)} %all_to_all.23), calls=%async_computation | async-start | bytes 16384 | tf_op jit(solution)/shard_map/all_to_all | solution.py:40
  54.3 93.0 %all-to-all-start.2 = ((bf16[16,72,2048]{2,1,0:T(8,128)(2,1)}), bf16[16,72,2048]{2,1,0:T(8,128)(2,1)}, u32[]{:S(2)}, u32[]{:S(2)}) async-start(bf16[16,72,2048]{2,1,0:T(8,128)(2,1)} %bitcast.85), calls=%async_computation.2 | async-start | bytes 9437184 | tf_op jit(solution)/shard_map/all_to_all | solution.py:38
  147.3 108.6 %all-to-all-start.1 = ((bf16[16,72,2048]{2,1,0:T(8,128)(2,1)}), bf16[16,72,2048]{2,1,0:T(8,128)(2,1)}, u32[]{:S(2)}, u32[]{:S(2)}) async-start(bf16[16,72,2048]{2,1,0:T(8,128)(2,1)} %bitcast.84), calls=%async_computation.1 | async-start | bytes 9437184 | tf_op jit(solution)/shard_map/all_to_all | solution.py:39
  169.1 348.1 %reduce-scatter.2.cloned.1.call-start = ((), (), s32[]{:S(2)}) async-start(), calls=%async_computation.6 | async-start | bytes 14155776 | tf_op jit(solution)/shard_map/reduce_scatter | solution.py:83
  255.9 5.2 copy-start.7
  266.9 5.4 copy-start.5
  266.9 10.2 %copy-start.4 = (bf16[1,1152,384]{1,2,0:T(8,128)(2,1)}, bf16[1,1152,384]{1,2,0:T(8,128)(2,1)S(1)}, u32[]{:S(2)}) copy-start(bf16[1,1152,384]{1,2,0:T(8,128)(2,1)S(1)} %get-tuple-element.25) | copy-start | bytes 2654212
  288.8 101.5 %all-to-all-start.4 = ((bf16[1,16,72]{2,0,1:T(2,128)(2,1)}), bf16[1,16,72]{2,0,1:T(2,128)(2,1)S(1)}, u32[]{:S(2)}, u32[]{:S(2)}) async-start(bf16[1,16,72]{2,0,1:T(2,128)(2,1)} %all_to_all.24), calls=%async_computation.4 | async-start | bytes 16384 | tf_op jit(solution)/shard_map/all_to_all | solution.py:68
  310.8 4.2 copy-start.6
  390.3 93.2 %all-to-all-start.3 = ((bf16[16,2,73728]{2,1,0:T(2,128)(2,1)}), bf16[16,2,73728]{2,1,0:T(2,128)(2,1)}, u32[]{:S(2)}, u32[]{:S(2)}) async-start(bf16[16,2,73728]{2,1,0:T(2,128)(2,1)} %reshape.393), calls=%async_computation.3 | async-start | bytes 9437184 | tf_op jit(solution)/shard_map/all_to_all | solution.py:67
  517.1 4.3 copy-start.2
  517.1 66.5 %copy-start.3 = (bf16[1,3,1024,384]{3,2,1,0:T(8,128)(2,1)S(1)}, bf16[1,3,1024,384]{3,2,1,0:T(8,128)(2,1)}, u32[]{:S(2)}) copy-start(bf16[1,3,1024,384]{3,2,1,0:T(8,128)(2,1)} %param.12) | copy-start | bytes 7077892
  583.6 7.8 %copy-start.1 = (bf16[128,2048]{1,0:T(8,128)(2,1)S(1)}, bf16[128,2048]{1,0:T(8,128)(2,1)}, u32[]{:S(2)}) copy-start(bf16[128,2048]{1,0:T(8,128)(2,1)} %param.7) | copy-start | bytes 1572868
Sparse Core Ops, SparseCore 0:
  286.8 127.6 reduce-scatter.1
where the time goes:
time: 604 us; the launch traced here: 599 us
  waiting for transfers between devices  223 us (37%)
  local copies, waits for them, and re-layouts  141 us (23%)
  starting transfers between devices  64 us (11%)
  blocking collectives  57.8 us (10%)
  other arithmetic  56.8 us (9%)
  matrix products  41 us (7%)
  between operations  15.5 us (3%)
    all_to_all x1, waiting for transfers between devices, on_device(): lax.all_to_all(send_cot, 'ep', split_axis=0, concat_axis=1, tiled=True)  80.3 us
    all_to_all x1, waiting for transfers between devices, on_device(): lax.all_to_all(slot_back, 'ep', split_axis=1, concat_axis=0, tiled=True)  79.1 us
    all_to_all x1, waiting for transfers between devices, on_device(): lax.all_to_all(send_tokens, 'ep', split_axis=0, concat_axis=1, tiled=True)  63.4 us
    psum x1, blocking collectives, on_device(): square_sum = lax.psum(jnp.sum(grad_share * grad_share), ('dp', 'ep'))  57.8 us
    unnamed x23, local copies, waits for them, and re-layouts  37.8 us
    unnamed x1, other arithmetic  29.9 us
    optimization_barrier x1, local copies, waits for them, and re-layouts, on_device(): slot_back = lax.optimization_barrier(slot_back.astype(jnp.bfloat16))  27.6 us
    scatter x1, local copies, waits for them, and re-layouts, on_device(): send_cot = jnp.zeros((experts * capacity, model_width), jnp.bfloat16).at[...  23.4 us
  transfers between devices with their start and end apart: 6, of which 3 were waited for; matrix products, arithmetic and copies ran while one was open for 29% of the time, Pallas kernels for 0%

commit v1 on v0

--- a/solution.py
+++ b/solution.py
@@ -102,6 +102,97 @@
     )
 
 
+def finish(grad_share, first_moment, second_moment, param_count):
+    square_sum = lax.psum(jnp.sum(grad_share * grad_share), ("dp", "ep"))
+    root_mean = jnp.sqrt(square_sum / param_count + 1e-06)
+    clip_factor = jnp.minimum(1.0, 0.5 / root_mean)
+    clipped = clip_factor * grad_share
+    first_next = 0.9 * first_moment.astype(jnp.float32) + 0.1 * clipped
+    second_next = 0.95 * second_moment.astype(jnp.float32) + 0.05 * clipped * clipped
+    update = (
+        first_next
+        / (1.0 - 0.9**ADAM_STEP)
+        / (jnp.sqrt(second_next / (1.0 - 0.95**ADAM_STEP)) + 1e-08)
+    )
+    return (
+        first_next.astype(jnp.bfloat16),
+        second_next.astype(jnp.bfloat16),
+        update.astype(jnp.bfloat16),
+    )
+
+
+def on_device_gather(
+    tokens, cotangent, expert_ids, route_weights, weights, first_moment, second_moment
+):
+    f32, bf16 = jnp.float32, jnp.bfloat16
+    tok_count, model_width = tokens.shape
+    topk_count = expert_ids.shape[1]
+    hidden_units = weights.shape[3]
+    groups = lax.axis_size("ep")
+    experts = groups
+    capacity = (tok_count * topk_count * 9 + 8 * experts - 1) // (8 * experts)
+    rows = groups * capacity
+    named = expert_ids[:, :, None] == jnp.arange(experts, dtype=jnp.int32)[None, None, :]
+    table = jnp.sum(jnp.where(named, route_weights.astype(f32)[:, :, None], 0.0), 1).T.astype(bf16)
+    mine = lax.all_to_all(table, "ep", split_axis=0, concat_axis=0, tiled=True)
+    x_all = lax.all_gather(tokens, "ep")
+    cot_all = lax.all_gather(cotangent, "ep")
+    routed = mine > 0
+    position = jnp.cumsum(routed.astype(jnp.int32), 1) - 1
+    slots = jnp.arange(capacity, dtype=jnp.int32)
+    pick = ((position[:, None, :] == slots[None, :, None]) & routed[:, None, :]).astype(bf16)
+    recv_x = jnp.einsum("bst,btd->bsd", pick, x_all, preferred_element_type=f32).astype(bf16)
+    recv_cot = jnp.einsum("bst,btd->bsd", pick, cot_all, preferred_element_type=f32).astype(bf16)
+    recv_weight = jnp.sum(pick.astype(f32) * mine.astype(f32)[:, None, :], 2)
+    recv_x = recv_x.reshape(rows, model_width)
+    recv_cot = recv_cot.reshape(rows, model_width)
+    row_weight = recv_weight.reshape(rows, 1)
+    w_gate, w_up, w_down = weights[0, 0], weights[0, 1], weights[0, 2]
+    gate_val = jnp.dot(recv_x, w_gate, preferred_element_type=f32)
+    up_val = jnp.dot(recv_x, w_up, preferred_element_type=f32)
+    sigmoid_gate = jax.nn.sigmoid(gate_val)
+    activated = gate_val * sigmoid_gate
+    hidden = lax.optimization_barrier((activated * up_val).astype(bf16))
+    back_val = jnp.dot(recv_cot, w_down, preferred_element_type=f32)
+    route_part = jnp.sum(hidden.astype(f32) * back_val, 1).astype(bf16)
+    scaled = row_weight * back_val
+    dgate = (scaled * up_val * sigmoid_gate * (1.0 + gate_val * (1.0 - sigmoid_gate))).astype(bf16)
+    dup = (scaled * activated).astype(bf16)
+    down_cot = (row_weight * recv_cot.astype(f32)).astype(bf16)
+    by_row = (((0,), (0,)), ((), ()))
+    grads = [
+        lax.dot_general(recv_x, dgate, by_row, preferred_element_type=f32),
+        lax.dot_general(recv_x, dup, by_row, preferred_element_type=f32),
+        lax.dot_general(down_cot, hidden, by_row, preferred_element_type=f32),
+    ]
+    half = model_width // 2
+    part = lax.axis_index("dp")
+    kept = jnp.stack([lax.dynamic_slice_in_dim(g, part * half, half, 0) for g in grads])
+    sent = jnp.stack([lax.dynamic_slice_in_dim(g, (1 - part) * half, half, 0) for g in grads])
+    got = lax.ppermute(sent.astype(bf16), "dp", [(0, 1), (1, 0)])
+    by_col = (((1,), (1,)), ((), ()))
+    slot_back = lax.dot_general(dgate, w_gate, by_col, preferred_element_type=f32)
+    slot_back = slot_back + lax.dot_general(dup, w_up, by_col, preferred_element_type=f32)
+    slot_back = slot_back.astype(bf16).reshape(groups, capacity, model_width)
+    spread = jnp.einsum("bst,bsd->btd", pick, slot_back, preferred_element_type=f32).astype(bf16)
+    token_grad = lax.psum_scatter(spread, "ep", scatter_dimension=0)
+    route_rows = jnp.sum(
+        pick.astype(f32) * route_part.astype(f32).reshape(groups, capacity, 1), 1
+    ).astype(bf16)
+    route_back = lax.all_to_all(route_rows, "ep", split_axis=0, concat_axis=0, tiled=True)
+    routing_grad = jnp.sum(
+        jnp.where(named, route_back.T.astype(f32)[:, None, :], 0.0), 2
+    ).astype(bf16)
+    grad_share = (kept + got.astype(f32))[None]
+    return (token_grad, routing_grad) + finish(
+        grad_share, first_moment, second_moment, 3.0 * experts * model_width * hidden_units
+    )
+
+
+def fits(mesh):
+    return mesh.shape["dp"] == 2 and mesh.shape["ep"] <= 16
+
+
 def solution(mesh):
     in_specs = (
         P(("dp", "ep"), None),
@@ -120,5 +211,5 @@
         P("ep", None, "dp", None),
     )
     return jax.shard_map(
-        on_device, mesh=mesh, in_specs=in_specs, out_specs=out_specs, check_vma=False
-    )
+        on_device_gather if fits(mesh) else on_device, mesh=mesh, in_specs=in_specs, out_specs=out_specs, check_vma=False
+    )

time: 604 us -> 326 us (0.54)
  local copies, waits for them, and re-layouts: 141 us -> 6.85 us
  starting transfers between devices: 64 us -> 5.01 us
  waiting for transfers between devices: 223 us -> 177 us
  other arithmetic: 56.8 us -> 20.5 us
  matrix products: 41 us -> 47.1 us
    all_to_all x5 -> x1, waiting for transfers between devices: 223 us -> 1.97 us  [on_device_gather(): lax.all_to_all(route_rows, 'ep', split_axis=0, concat_axis=0, tiled=True)]
    all_gather x0 -> x2, waiting for transfers between devices: none -> 132 us  [the longest x1 68.4 us: on_device_gather(): cot_all = lax.all_gather(cotangent, 'ep')]
    all_to_all x5 -> x1, starting transfers between devices: 64 us -> 3.47 us  [on_device_gather(): lax.all_to_all(route_rows, 'ep', split_axis=0, concat_axis=0, tiled=True)]
    scatter x3 -> x0, local copies, waits for them, and re-layouts: 54.3 us -> none  [the longest x1 23.4 us: on_device(): send_cot = jnp.zeros((experts * capacity, model_width), jnp.bfloat16).at[...]
    ppermute x0 -> x1, waiting for transfers between devices: none -> 41.9 us  [on_device_gather(): got = lax.ppermute(sent.astype(bf16), 'dp', [(0, 1), (1, 0)])]
    unnamed x23 -> x24, local copies, waits for them, and re-layouts: 37.8 us -> 2.13 us
    unnamed x1 -> x2, other arithmetic: 29.9 us -> 0.01 us
    optimization_barrier x1 -> x0, local copies, waits for them, and re-layouts: 27.6 us -> none  [on_device(): slot_back = lax.optimization_barrier(slot_back.astype(jnp.bfloat16))]
  transfers between devices with their start and end apart: 6 -> 5, of which waited for: 3 -> 4; matrix products, arithmetic and copies ran while one was open for 29% -> 12% of each run, Pallas kernels for 0% -> 0%
where the time goes in v1:
time: 326 us
  waiting for transfers between devices  177 us (54%)
  blocking collectives  54.3 us (17%)
  matrix products  47.1 us (14%)
  other arithmetic  20.5 us (6%)
  between operations  14.7 us (5%)
  local copies, waits for them, and re-layouts  6.85 us (2%)
  starting transfers between devices  5.01 us (2%)
    all_gather x1, waiting for transfers between devices, on_device_gather(): cot_all = lax.all_gather(cotangent, 'ep')  68.4 us
    all_gather x1, waiting for transfers between devices, on_device_gather(): x_all = lax.all_gather(tokens, 'ep')  63.8 us
    ppermute x1, waiting for transfers between devices, on_device_gather(): got = lax.ppermute(sent.astype(bf16), 'dp', [(0, 1), (1, 0)])  41.9 us
    psum x1, blocking collectives, finish(): square_sum = lax.psum(jnp.sum(grad_share * grad_share), ('dp', 'ep'))  40.7 us
    all_to_all x1, blocking collectives, on_device_gather(): mine = lax.all_to_all(table, 'ep', split_axis=0, concat_axis=0, tiled=True)  13.6 us
    convert_element_type x1, other arithmetic, finish(): update.astype(jnp.bfloat16)  8.23 us
    dot_general x1, matrix products, on_device_gather(): jnp.einsum('bst,btd->bsd', pick, x_all, preferred_element_type=f32)  6.94 us
  transfers between devices with their start and end apart: 5, of which 4 were waited for; matrix products, arithmetic and copies ran while one was open for 12% of the time, Pallas kernels for 0%

profile of v1, /device:TPU:0, one launch (start us, length us, event | category | flops | bytes accessed | tf_op | source)
XLA Modules:
  0.0 326.0 jit_solution(8635559303250219173)
XLA Ops:
  7.2 0.0 all-gather.7.cloned.1.call-start
  7.2 0.7 all-gather.7.cloned.1.call-update
  7.9 0.0 all-gather.5.cloned.1.call-start
  7.9 0.7 all-gather.5.cloned.1.call-update
  8.6 0.0 reduce-scatter.2.cloned.1.call-start
  8.7 0.7 convert_element_type.112
  9.4 0.7 select_reduce_fusion.1
  10.1 13.6 %all_to_all.15 = bf16[16,1,128]{2,1,0:T(2,128)(2,1)S(1)} all-to-all(bf16[16,1,128]{2,1,0:T(2,128)(2,1)S(1)} %copy.39), channel_id=1, replica_groups=mesh['dp'=2,'ep'=16] {'ep'}, dimensions={0} | all-to-all | bytes 8192 | tf_op jit(solution)/shard_map/all_to_all | solution.py:137
  23.7 0.3 reduce_window_sum.17
  24.0 63.8 %all-gather.7.cloned.1.call-done = bf16[2048,2048]{1,0:T(8,128)(2,1)} async-done(((bf16[128,2048]{1,0:T(8,128)(2,1)}), bf16[2048,2048]{1,0:T(8,128)(2,1)}) %all-gather.7.cloned.1.call-update) | async-done | bytes 8388624 | tf_op jit(solution)/shard_map/all_gather | solution.py:138
  87.8 6.9 %convolution_convert_fusion.1 = bf16[16,72,2048]{2,1,0:T(8,128)(2,1)} fusion(bf16[16,128,2048]{2,1,0:T(8,128)(2,1)} %bitcast.77, s32[16,128]{1,0:T(8,128)S(1)} %broadcast_add_fusion, pred[16,128]{1,0:T(8,128)(4,1)S(1)} %get-tuple-element.8), kind=kOutput, calls=%fused_computation.13 | convolution fusion | flops 606633984 | bytes 13117440 | tf_op jit(solution)/shard_map/bst,btd->bsd/dot_general | solution.py:144
  94.7 68.4 %all-gather.5.cloned.1.call-done = bf16[2048,2048]{1,0:T(8,128)(2,1)} async-done(((bf16[128,2048]{1,0:T(8,128)(2,1)}), bf16[2048,2048]{1,0:T(8,128)(2,1)}) %all-gather.5.cloned.1.call-update) | async-done | bytes 8388624 | tf_op jit(solution)/shard_map/all_gather | solution.py:139
  163.1 4.9 %convolution_convert_fusion.2 = bf16[16,72,2048]{2,1,0:T(8,128)(2,1)S(1)} fusion(bf16[16,128,2048]{2,1,0:T(8,128)(2,1)} %bitcast.78, s32[16,128]{1,0:T(8,128)S(1)} %broadcast_add_fusion, pred[16,128]{1,0:T(8,128)(4,1)S(1)} %get-tuple-element.8), kind=kOutput, calls=%fused_computation.14 | convolution fusion | flops 606633984 | bytes 13117440 | tf_op jit(solution)/shard_map/bst,btd->bsd/dot_general | solution.py:145
  168.1 1.2 slice-done.3
  169.3 2.4 fusion.10
  171.7 0.0 copy-start.2
  171.7 3.8 %multiply_convert_fusion.2 = (bf16[1152,384]{0,1:T(8,128)(2,1)S(1)}, f32[1152,384]{0,1:T(8,128)}) fusion(f32[1152,384]{0,1:T(8,128)S(1)} %fusion.10, bf16[1152,2048]{1,0:T(8,128)(2,1)S(1)} %bitcast.81, bf16[1,3,2048,384]{3,2,1,0:T(8,128)(2,1)S(1)} %bitcast.89), kind=kOutput, calls=%fused_computation.19 | convolution fusion | flops 1814593536 | bytes 10715136 | tf_op jit(solution)/shard_map/dot_general | solution.py:152
  175.5 3.6 %multiply_reduce_fusion.1 = (bf16[1152]{0:T(1024)(128)(2,1)S(1)}, f32[1152,384]{0,1:T(8,128)}) fusion(bf16[1152,384]{0,1:T(8,128)(2,1)S(1)} %get-tuple-element.14, bf16[1152,2048]{1,0:T(8,128)(2,1)S(1)} %bitcast.86, bf16[1,3,2048,384]{3,2,1,0:T(8,128)(2,1)S(1)} %bitcast.89), kind=kOutput, calls=%fused_computation.18 | convolution fusion | flops 1813265280 | bytes 8947968 | tf_op jit(solution)/shard_map/dot_general | solution.py:156
  179.1 0.1 reshape.65
  179.2 0.6 fusion.26
  179.8 0.1 mul.122
  179.8 3.4 %multiply_convert_fusion.3 = (bf16[1152,384]{0,1:T(8,128)(2,1)S(1)}, bf16[1152,384]{0,1:T(8,128)(2,1)S(1)}) fusion(f32[1152,384]{0,1:T(8,128)} %get-tuple-element.17, f32[1152]{0:T(1024)S(1)} %mul.122, f32[1152,384]{0,1:T(8,128)} %copy-done.2, f32[1152,384]{0,1:T(8,128)} %get-tuple-element.15), kind=kLoop, calls=%fused_computation.20 | loop fusion | flops 6193152 | bytes 7082496 | tf_op jit(solution)/shard_map/convert_element_type | solution.py:160
  183.3 4.3 %fusion.8 = f32[1152,2048]{1,0:T(8,128)S(1)} fusion(bf16[1152,384]{0,1:T(8,128)(2,1)S(1)} %get-tuple-element.13, bf16[1,3,2048,384]{3,2,1,0:T(8,128)(2,1)} %param.11), kind=kOutput, calls=%fused_computation.24 | convolution fusion | flops 1811939328 | bytes 11894784 | tf_op jit(solution)/shard_map/dot_general | solution.py:174
  187.6 4.1 %fusion = bf16[1152,2048]{1,0:T(8,128)(2,1)S(1)} fusion(f32[1152,2048]{1,0:T(8,128)S(1)} %fusion.8, bf16[1152,384]{0,1:T(8,128)(2,1)S(1)} %get-tuple-element.12, bf16[1,3,2048,384]{3,2,1,0:T(8,128)(2,1)} %param.11), kind=kOutput, calls=%fused_computation.2 | convolution fusion | flops 1816657920 | bytes 16613376 | tf_op jit(solution)/shard_map/dot_general | solution.py:175
  191.6 5.6 %convolution_convert_fusion = bf16[16,128,2048]{2,1,0:T(8,128)(2,1)} fusion(bf16[16,72,2048]{2,1,0:T(8,128)(2,1)S(1)} %bitcast.79, s32[16,128]{1,0:T(8,128)S(1)} %broadcast_add_fusion, pred[16,128]{1,0:T(8,128)(4,1)S(1)} %get-tuple-element.8), kind=kOutput, calls=%fused_computation.4 | convolution fusion | flops 608468992 | bytes 13117440 | tf_op jit(solution)/shard_map/bst,bsd->btd/dot_general | solution.py:177
  197.3 0.0 reduce-scatter.2.cloned.1.call-update
  197.3 0.0 slice-start.1
  197.3 5.7 %fusion.3 = f32[2048,384]{1,0:T(8,128)S(1)} fusion(bf16[1152,384]{0,1:T(8,128)(2,1)S(1)} %get-tuple-element.14, bf16[1152,2048]{1,0:T(8,128)(2,1)} %bitcast.87, f32[1152]{0:T(1024)S(1)} %mul.122), kind=kOutput, calls=%fused_computation.7 | convolution fusion | flops 1819017216 | bytes 8753664 | tf_op jit(solution)/shard_map/dot_general | solution.py:166
  203.0 0.1 fusion.24
  203.1 0.0 slice-done
  203.2 0.0 slice-done.1
  203.2 2.9 fusion.40
  206.1 2.9 fusion.39
  209.0 0.2 fusion.22
  209.2 2.0 pad_maximum_fusion
  211.3 0.2 copy-done.5
  211.5 1.4 collective-permute-start
  212.9 0.6 copy.46
  213.5 3.5 %all-to-all-start.1 = ((bf16[16,1,128]{2,1,0:T(2,128)(2,1)}), bf16[16,1,128]{2,1,0:T(2,128)(2,1)S(1)}, u32[]{:S(2)}, u32[]{:S(2)}) async-start(bf16[16,1,128]{2,1,0:T(2,128)(2,1)} %copy.46), calls=%async_computation.2 | async-start | bytes 16384 | tf_op jit(solution)/shard_map/all_to_all | solution.py:182
  217.0 2.4 dynamic-slice_bitcast_fusion
  219.4 0.7 copy-done.6
  220.0 1.3 dynamic-slice_bitcast_fusion.2
  221.3 2.0 all-to-all-done.1
  223.3 41.9 %collective-permute-done = bf16[3,1024,384]{2,1,0:T(8,128)(2,1)} collective-permute-done((bf16[3,1024,384]{2,1,0:T(8,128)(2,1)}, bf16[3,1024,384]{2,1,0:T(8,128)(2,1)}, u32[]{:S(2)}, u32[]{:S(2)}) %collective-permute-start) | collective-permute-done | bytes 2359328 | tf_op jit(solution)/shard_map/ppermute | solution.py:172
  265.2 4.0 %multiply_reduce_fusion = f32[]{:T(128)} fusion(bf16[3,1024,384]{2,1,0:T(8,128)(2,1)} %collective-permute-done, f32[1,1024,384]{2,1,0:T(8,128)S(1)} %get-tuple-element.20, f32[1,1024,384]{2,1,0:T(8,128)S(1)} %get-tuple-element.21, f32[1,1024,384]{2,1,0:T(8,128)} %dynamic-slice_bitcast_fusion.2), kind=kLoop, calls=%fused_computation.11 | loop fusion | flops 7077887 | bytes 7077892 | tf_op jit(solution)/shard_map/reduce_sum | solution.py:106
  269.2 0.6 select_reduce_fusion
  269.8 40.7 %psum.7 = f32[]{:T(128)} all-reduce(f32[]{:T(128)} %multiply_reduce_fusion), channel_id=1, replica_groups=mesh['dp'=2,'ep'=16] {'dp','ep'}, use_global_device_ids=true, to_apply=%region_8.9 | all-reduce | flops 1 | bytes 8 | tf_op jit(solution)/shard_map/psum | solution.py:106
  311.3 8.2 %divide_convert_fusion = (bf16[1,3,1024,384]{3,2,1,0:T(8,128)(2,1)}, bf16[1,3,1024,384]{3,2,1,0:T(8,128)(2,1)}, bf16[1,3,1024,384]{3,2,1,0:T(8,128)(2,1)}) fusion(bf16[1,3,1024,384]{3,2,1,0:T(8,128)(2,1)} %param.12, bf16[1,3,1024,384]{3,2,1,0:T(8,128)(2,1)} %param.13, f32[]{:T(128)S(6)} %min.3, bf16[3,1024,384]{2,1,0:T(8,128)(2,1)} %collective-permute-done, ...), kind=kLoop, calls=%fused_computation.10 | loop fusion | flops 24772608 | bytes 18874372 | tf_op jit(solution)/shard_map/convert_element_type | solution.py:120
  (25 shorter events, 0.1 us)
Async XLA Ops:
  7.2 80.6 %all-gather.7.cloned.1.call-start = ((), (), s32[]{:S(2)}) async-start(), calls=%async_computation.5 | async-start | bytes 8912896 | tf_op jit(solution)/shard_map/all_gather | solution.py:138
  7.9 155.2 %all-gather.5.cloned.1.call-start = ((), (), s32[]{:S(2)}) async-start(), calls=%async_computation.4 | async-start | bytes 8912896 | tf_op jit(solution)/shard_map/all_gather | solution.py:139
  8.6 310.8 %reduce-scatter.2.cloned.1.call-start = ((), (), s32[]{:S(2)}) async-start(), calls=%async_computation.3 | async-start | bytes 8912896 | tf_op jit(solution)/shard_map/reduce_scatter | solution.py:178
  87.8 80.3 %slice-start.2 = ((s8[4718592]{0:T(1024)(128)(4,1)}), s8[524288]{0:T(1024)(128)(4,1)S(1)}, s32[]{:S(2)}) async-start(s8[4718592]{0:T(1024)(128)(4,1)} %bitcast.88), calls=%async_computation.8 | async-start | bytes 1048576
  163.1 4.9 %copy-start = (bf16[16,72,2048]{2,1,0:T(8,128)(2,1)S(1)}, bf16[16,72,2048]{2,1,0:T(8,128)(2,1)}, u32[]{:S(2)}) copy-start(bf16[16,72,2048]{2,1,0:T(8,128)(2,1)} %convolution_convert_fusion.1) | copy-start | bytes 14155780
  163.1 6.2 %slice-start.3 = ((s8[4718592]{0:T(1024)(128)(4,1)}), s8[4194304]{0:T(1024)(128)(4,1)S(1)}, s32[]{:S(2)}) async-start(s8[4718592]{0:T(1024)(128)(4,1)} %bitcast.88), calls=%async_computation.9 | async-start | bytes 8388608
  168.1 7.4 %copy-start.1 = (bf16[16,72,2048]{2,1,0:T(8,128)(2,1)}, bf16[16,72,2048]{2,1,0:T(8,128)(2,1)S(1)}, u32[]{:S(2)}) copy-start(bf16[16,72,2048]{2,1,0:T(8,128)(2,1)S(1)} %convolution_convert_fusion.2) | copy-start | bytes 14155780
  171.7 3.8 %copy-start.2 = (f32[1152,384]{0,1:T(8,128)}, f32[1152,384]{0,1:T(8,128)S(1)}, u32[]{:S(2)}) copy-start(f32[1152,384]{0,1:T(8,128)S(1)} %fusion.10) | copy-start | bytes 5308420
  197.3 5.9 %slice-start = ((s8[4718592]{0:T(1024)(128)(4,1)}), s8[524288]{0:T(1024)(128)(4,1)S(1)}, s32[]{:S(2)}) async-start(s8[4718592]{0:T(1024)(128)(4,1)} %bitcast.82), calls=%async_computation.6 | async-start | bytes 1048576
  197.3 5.8 %slice-start.1 = ((s8[4718592]{0:T(1024)(128)(4,1)}), s8[4194304]{0:T(1024)(128)(4,1)S(1)}, s32[]{:S(2)}) async-start(s8[4718592]{0:T(1024)(128)(4,1)} %bitcast.82), calls=%async_computation.7 | async-start | bytes 8388608
  203.0 3.1 copy-start.3
  206.1 2.9 copy-start.4
  209.0 2.5 copy-start.5
  211.5 53.7 %collective-permute-start = (bf16[3,1024,384]{2,1,0:T(8,128)(2,1)}, bf16[3,1024,384]{2,1,0:T(8,128)(2,1)}, u32[]{:S(2)}, u32[]{:S(2)}) collective-permute-start(bf16[3,1024,384]{2,1,0:T(8,128)(2,1)} %pad_maximum_fusion), channel_id=1, source_target_pairs={{0,16},{16,0},{1,17},{17,1},{2,18},{18,2},{3,19},{19,3},{4,20},{20... | collective-permute-start | bytes 7077896 | tf_op jit(solution)/shard_map/ppermute | solution.py:172
  213.5 9.8 %all-to-all-start.1 = ((bf16[16,1,128]{2,1,0:T(2,128)(2,1)}), bf16[16,1,128]{2,1,0:T(2,128)(2,1)S(1)}, u32[]{:S(2)}, u32[]{:S(2)}) async-start(bf16[16,1,128]{2,1,0:T(2,128)(2,1)} %copy.46), calls=%async_computation.2 | async-start | bytes 16384 | tf_op jit(solution)/shard_map/all_to_all | solution.py:182
  217.0 3.0 copy-start.6
  220.0 49.2 %copy-start.7 = (s32[128,8]{0,1:T(8,128)S(1)}, s32[128,8]{0,1:T(8,128)}, u32[]{:S(2)}) copy-start(s32[128,8]{0,1:T(8,128)} %param.9) | copy-start | bytes 12292
Sparse Core Ops, SparseCore 0:
  10.2 77.5 all-gather.6
  90.0 73.1 all-gather.4
  197.4 103.8 reduce-scatter.1

commit v2 on v1

--- a/solution.py
+++ b/solution.py
@@ -1,6 +1,10 @@
+import functools
+
 import jax
 import jax.numpy as jnp
 from jax import lax
+from jax.experimental import pallas as pl
+from jax.experimental.pallas import tpu as pltpu
 from jax.sharding import PartitionSpec as P
 
 ADAM_STEP = 10
@@ -121,6 +125,360 @@
     )
 
 
+MESH = pl.DeviceIdType.MESH
+MIB = 1024 * 1024
+
+
+def place(groups):
+    me = lax.axis_index("ep")
+    core = lax.rem(me, 2)
+    side = lax.rem(me // 2, 2)
+    return me // 4, side, core, groups // 4
+
+
+def index_of(z, y, core):
+    return (z * 2 + y) * 2 + core
+
+
+def greet(z, y, core, depth, partner):
+    barrier = pltpu.get_barrier_semaphore()
+
+    def hello(device):
+        pl.semaphore_signal(barrier, inc=1, device_id=device, device_id_type=MESH)
+
+    hello({"ep": index_of(z, y, 1 - core)})
+    hello({"ep": index_of(z, 1 - y, core)})
+    expected = 2
+    if partner is not None:
+        hello(partner)
+        expected = 3
+
+    @pl.when(z > 0)
+    def _():
+        hello({"ep": index_of(z - 1, y, core)})
+
+    @pl.when(z < depth - 1)
+    def _():
+        hello({"ep": index_of(z + 1, y, core)})
+
+    pl.semaphore_wait(
+        barrier, expected + jnp.where(z > 0, 1, 0) + jnp.where(z < depth - 1, 1, 0)
+    )
+
+
+def gather_kernel(groups, x_ref, c_ref, t_ref, xs, cs, ts, up_sem, down_sem, y_sem, core_sem, recv_sem, own_sem):
+    z, y, core, depth = place(groups)
+    me = index_of(z, y, core)
+    arrays = ((x_ref, xs), (c_ref, cs), (t_ref, ts))
+    greet(z, y, core, depth, None)
+
+    def copies(block, source_own, sems, slot, device):
+        return [
+            pltpu.make_async_remote_copy(
+                src_ref=own if source_own else full.at[block],
+                dst_ref=full.at[block],
+                send_sem=sems.at[i, slot],
+                recv_sem=recv_sem.at[i, block],
+                device_id={"ep": device},
+                device_id_type=MESH,
+            )
+            for i, (own, full) in enumerate(arrays)
+        ]
+
+    def start(block, source_own, sems, slot, device):
+        for copy in copies(block, source_own, sems, slot, device):
+            copy.start()
+
+    def arrived(block):
+        for copy in copies(block, False, core_sem, 0, index_of(z, y, 1 - core)):
+            copy.wait_recv()
+
+    local = [
+        pltpu.make_async_copy(own, full.at[me], own_sem.at[i])
+        for i, (own, full) in enumerate(arrays)
+    ]
+    above, below = index_of(z + 1, y, core), index_of(z - 1, y, core)
+    beside, sibling = index_of(z, 1 - y, core), index_of(z, y, 1 - core)
+
+    @pl.when(z < depth - 1)
+    def _():
+        start(me, True, up_sem, z, above)
+
+    @pl.when(z > 0)
+    def _():
+        start(me, True, down_sem, z, below)
+
+    start(me, True, y_sem, z, beside)
+    start(me, True, core_sem, z * 2 + y, sibling)
+    for copy in local:
+        copy.start()
+
+    def pass_on(level, side):
+        block = index_of(level, side, core)
+        arrived(block)
+        start(block, False, core_sem, level * 2 + side, sibling)
+        return block
+
+    for step in range(1, depth):
+        @pl.when(z - step >= 0)
+        def _():
+            level = z - step
+            block = index_of(level, y, core)
+            arrived(block)
+
+            @pl.when(z < depth - 1)
+            def _():
+                start(block, False, up_sem, level, above)
+
+            start(block, False, y_sem, level, beside)
+            start(block, False, core_sem, level * 2 + y, sibling)
+
+        @pl.when(z + step <= depth - 1)
+        def _():
+            level = z + step
+            block = index_of(level, y, core)
+            arrived(block)
+
+            @pl.when(z > 0)
+            def _():
+                start(block, False, down_sem, level, below)
+
+            start(block, False, y_sem, level, beside)
+            start(block, False, core_sem, level * 2 + y, sibling)
+
+        if step == 1:
+            pass_on(z, 1 - y)
+
+        @pl.when(z - step >= 0)
+        def _():
+            pass_on(z - step, 1 - y)
+
+        @pl.when(z + step <= depth - 1)
+        def _():
+            pass_on(z + step, 1 - y)
+
+    for level in range(depth):
+        for side in range(2):
+            arrived(index_of(level, side, 1 - core))
+    for copy in local:
+        copy.wait()
+
+    def sent(sems, slot, device):
+        for copy in copies(me, True, sems, slot, device):
+            copy.wait_send()
+
+    for level in range(depth):
+        @pl.when((z < depth - 1) & (level <= z))
+        def _():
+            sent(up_sem, level, above)
+
+        @pl.when((z > 0) & (level >= z))
+        def _():
+            sent(down_sem, level, below)
+
+        sent(y_sem, level, beside)
+        for side in range(2):
+            sent(core_sem, level * 2 + side, sibling)
+
+
+def gather_blocks(tokens, cotangent, table, groups):
+    depth = groups // 4
+    any_space = pl.BlockSpec(memory_space=pl.ANY)
+    dma = pltpu.SemaphoreType.DMA
+    arrays = (tokens, cotangent, table)
+    return pl.pallas_call(
+        functools.partial(gather_kernel, groups),
+        out_shape=[jax.ShapeDtypeStruct((groups,) + a.shape, a.dtype) for a in arrays],
+        in_specs=[any_space] * 3,
+        out_specs=[any_space] * 3,
+        scratch_shapes=[
+            dma((3, depth)),
+            dma((3, depth)),
+            dma((3, depth)),
+            dma((3, 2 * depth)),
+            dma((3, groups)),
+            dma((3,)),
+        ],
+        compiler_params=pltpu.CompilerParams(
+            collective_id=1, has_side_effects=True, vmem_limit_bytes=48 * MIB
+        ),
+    )(*arrays)
+
+
+def combine_kernel(
+    groups, sp, rt, g_ref, out, route_out, g_got,
+    core_s, core_r, ys_s, ys_r, y_s, y_r, zs_s, zs_r, in_s, in_r,
+    core_send, core_recv, y_send, y_recv, z_send, z_recv, g_sem,
+):
+    z, y, core, depth = place(groups)
+    partner = {"dp": 1 - lax.axis_index("dp")}
+    greet(z, y, core, depth, partner)
+    g_copy = pltpu.make_async_remote_copy(
+        src_ref=g_ref, dst_ref=g_got, send_sem=g_sem.at[0], recv_sem=g_sem.at[1],
+        device_id=partner, device_id_type=MESH,
+    )
+    g_copy.start()
+    chunk = 16
+    chunks = sp.shape[1] // chunk
+    f32, bf16 = jnp.float32, jnp.bfloat16
+
+    def target(j):
+        if j == depth - 1:
+            return z
+        low = jnp.where(depth - 1 - j > z, depth - 1 - j, depth - 2 - j)
+        high = jnp.where(j < z, j, j + 1)
+        return jnp.where(z < depth // 2, low, high)
+
+    def pair(src, src_at, dst, dst_at, send, send_at, recv, recv_at, device):
+        return [
+            pltpu.make_async_remote_copy(
+                src_ref=src[i].at[src_at], dst_ref=dst[i].at[dst_at],
+                send_sem=send.at[i, send_at], recv_sem=recv.at[i, recv_at],
+                device_id={"ep": device}, device_id_type=MESH,
+            )
+            for i in range(2)
+        ]
+
+    def core_copy(level, side):
+        slot = level * 2 + side
+        return pair(
+            (sp, rt), index_of(level, side, 1 - core), (core_s, core_r), slot,
+            core_send, slot, core_recv, slot, index_of(z, y, 1 - core),
+        )
+
+    def y_copy(level):
+        return pair(
+            (ys_s, ys_r), level, (y_s, y_r), level,
+            y_send, level, y_recv, level, index_of(z, 1 - y, core),
+        )
+
+    def z_copy(level, going, slot):
+        return pair(
+            (zs_s, zs_r), level, (in_s, in_r), slot,
+            z_send, level, z_recv, slot, index_of(going, y, core),
+        )
+
+    def add(result, terms):
+        def body(i, carry):
+            rows = pl.ds(pl.multiple_of(i * chunk, chunk), chunk)
+            total = terms[0][0][terms[0][2], rows, :].astype(f32)
+            for term in terms[1:]:
+                total = total + term[0][term[2], rows, :].astype(f32)
+            if result[2] is None:
+                result[0][rows, :] = total.astype(bf16)
+            else:
+                result[0][result[2], rows, :] = total.astype(bf16)
+            return carry
+
+        lax.fori_loop(0, chunks, body, 0)
+        small = terms[0][1][terms[0][2]].astype(f32)
+        for term in terms[1:]:
+            small = small + term[1][term[2]].astype(f32)
+        if result[2] is None:
+            result[1][...] = small.astype(bf16)
+        else:
+            result[1][result[2]] = small.astype(bf16)
+
+    def each(copies, what):
+        for copy in copies:
+            getattr(copy, what)()
+
+    for side in (1 - y, y):
+        for j in range(depth):
+            each(core_copy(target(j), side), "start")
+    for j in range(depth):
+        t = target(j)
+        each(core_copy(t, 1 - y), "wait_recv")
+        add((ys_s, ys_r, t), [(sp, rt, index_of(t, 1 - y, core)), (core_s, core_r, t * 2 + 1 - y)])
+        each(y_copy(t), "start")
+    for j in range(depth - 1):
+        t = target(j)
+        each(core_copy(t, y), "wait_recv")
+        each(y_copy(t), "wait_recv")
+        terms = [(sp, rt, index_of(t, y, core)), (core_s, core_r, t * 2 + y), (y_s, y_r, t)]
+        upward = t > z
+        slot = jnp.where(upward, t, depth + t)
+        going = jnp.where(upward, z + 1, z - 1)
+        more = (upward & (z > 0)) | (jnp.logical_not(upward) & (z < depth - 1))
+
+        @pl.when(more)
+        def _():
+            each(z_copy(t, going, slot), "wait_recv")
+            add((zs_s, zs_r, t), terms + [(in_s, in_r, slot)])
+
+        @pl.when(jnp.logical_not(more))
+        def _():
+            add((zs_s, zs_r, t), terms)
+
+        each(z_copy(t, going, slot), "start")
+    each(core_copy(z, y), "wait_recv")
+    each(y_copy(z), "wait_recv")
+    terms = [(sp, rt, index_of(z, y, core)), (core_s, core_r, z * 2 + y), (y_s, y_r, z)]
+    from_below, from_above = (in_s, in_r, z), (in_s, in_r, depth + z)
+    beside = jnp.where(z > 0, z - 1, z + 1)
+
+    @pl.when(z > 0)
+    def _():
+        each(z_copy(z, beside, z), "wait_recv")
+
+    @pl.when(z < depth - 1)
+    def _():
+        each(z_copy(z, beside, depth + z), "wait_recv")
+
+    @pl.when((z > 0) & (z < depth - 1))
+    def _():
+        add((out, route_out, None), terms + [from_below, from_above])
+
+    @pl.when(z == 0)
+    def _():
+        add((out, route_out, None), terms + [from_above])
+
+    @pl.when(z == depth - 1)
+    def _():
+        add((out, route_out, None), terms + [from_below])
+
+    for j in range(depth):
+        t = target(j)
+        each(core_copy(t, 0), "wait_send")
+        each(core_copy(t, 1), "wait_send")
+        each(y_copy(t), "wait_send")
+        if j < depth - 1:
+            each(z_copy(t, beside, t), "wait_send")
+    g_copy.wait()
+
+
+def combine(spread, routes, sent, groups):
+    depth = groups // 4
+    bf16 = jnp.bfloat16
+    big, small = spread.shape[1:], routes.shape[1:]
+    vmem, any_space = pl.BlockSpec(memory_space=pltpu.VMEM), pl.BlockSpec(memory_space=pl.ANY)
+    dma = pltpu.SemaphoreType.DMA
+
+    def both(count):
+        return [pltpu.VMEM((count,) + big, bf16), pltpu.VMEM((count,) + small, bf16)]
+
+    return pl.pallas_call(
+        functools.partial(combine_kernel, groups),
+        out_shape=[
+            jax.ShapeDtypeStruct(big, bf16),
+            jax.ShapeDtypeStruct(small, bf16),
+            jax.ShapeDtypeStruct(sent.shape, bf16),
+        ],
+        in_specs=[vmem, vmem, any_space],
+        out_specs=[vmem, vmem, any_space],
+        scratch_shapes=both(2 * depth) + both(depth) + both(depth) + both(depth) + both(2 * depth)
+        + [
+            dma((2, 2 * depth)), dma((2, 2 * depth)),
+            dma((2, depth)), dma((2, depth)),
+            dma((2, depth)), dma((2, 2 * depth)),
+            dma((2,)),
+        ],
+        compiler_params=pltpu.CompilerParams(
+            collective_id=2, has_side_effects=True, vmem_limit_bytes=48 * MIB
+        ),
+    )(spread, routes, sent)
+
+
 def on_device_gather(
     tokens, cotangent, expert_ids, route_weights, weights, first_moment, second_moment
 ):
@@ -134,9 +492,9 @@
     rows = groups * capacity
     named = expert_ids[:, :, None] == jnp.arange(experts, dtype=jnp.int32)[None, None, :]
     table = jnp.sum(jnp.where(named, route_weights.astype(f32)[:, :, None], 0.0), 1).T.astype(bf16)
-    mine = lax.all_to_all(table, "ep", split_axis=0, concat_axis=0, tiled=True)
-    x_all = lax.all_gather(tokens, "ep")
-    cot_all = lax.all_gather(cotangent, "ep")
+    x_all, cot_all, tables = gather_blocks(tokens, cotangent, table, groups)
+    me = lax.axis_index("ep")
+    mine = lax.dynamic_slice_in_dim(tables, me, 1, 1)[:, 0, :]
     routed = mine > 0
     position = jnp.cumsum(routed.astype(jnp.int32), 1) - 1
     slots = jnp.arange(capacity, dtype=jnp.int32)
@@ -169,17 +527,17 @@
     part = lax.axis_index("dp")
     kept = jnp.stack([lax.dynamic_slice_in_dim(g, part * half, half, 0) for g in grads])
     sent = jnp.stack([lax.dynamic_slice_in_dim(g, (1 - part) * half, half, 0) for g in grads])
-    got = lax.ppermute(sent.astype(bf16), "dp", [(0, 1), (1, 0)])
     by_col = (((1,), (1,)), ((), ()))
     slot_back = lax.dot_general(dgate, w_gate, by_col, preferred_element_type=f32)
     slot_back = slot_back + lax.dot_general(dup, w_up, by_col, preferred_element_type=f32)
     slot_back = slot_back.astype(bf16).reshape(groups, capacity, model_width)
     spread = jnp.einsum("bst,bsd->btd", pick, slot_back, preferred_element_type=f32).astype(bf16)
-    token_grad = lax.psum_scatter(spread, "ep", scatter_dimension=0)
     route_rows = jnp.sum(
         pick.astype(f32) * route_part.astype(f32).reshape(groups, capacity, 1), 1
-    ).astype(bf16)
-    route_back = lax.all_to_all(route_rows, "ep", split_axis=0, concat_axis=0, tiled=True)
+    )
+    my_row = jnp.arange(experts, dtype=jnp.int32)[None, :, None] == me
+    routes = jnp.where(my_row, route_rows[:, None, :], 0.0).astype(bf16)
+    token_grad, route_back, got = combine(spread, routes, sent.astype(bf16), groups)
     routing_grad = jnp.sum(
         jnp.where(named, route_back.T.astype(f32)[:, None, :], 0.0), 2
     ).astype(bf16)
@@ -190,7 +548,7 @@
 
 
 def fits(mesh):
-    return mesh.shape["dp"] == 2 and mesh.shape["ep"] <= 16
+    return mesh.shape["dp"] == 2 and mesh.shape["ep"] == 16
 
 
 def solution(mesh):

time: 326 us -> 288 us (0.88)
  Pallas kernels: 0 us -> 182 us
  waiting for transfers between devices: 177 us -> 0 us
  blocking collectives: 54.3 us -> 38.6 us
  between operations: 14.7 us -> 1.6 us
  matrix products: 47.1 us -> 35.1 us
  local copies, waits for them, and re-layouts: 6.85 us -> 11.9 us
  starting transfers between devices: 5.01 us -> 0 us
    pallas_call x0 -> x2, Pallas kernels: none -> 182 us  [the longest x1 123 us: gather_blocks(): pl.pallas_call(functools.partial(gather_kernel, groups), out_shape=[jax.S...]
    all_gather x2 -> x0, waiting for transfers between devices: 132 us -> none  [the longest x1 68.4 us: on_device_gather(): cot_all = lax.all_gather(cotangent, 'ep')]
    ppermute x1 -> x0, waiting for transfers between devices: 41.9 us -> none  [on_device_gather(): got = lax.ppermute(sent.astype(bf16), 'dp', [(0, 1), (1, 0)])]
    all_to_all x1 -> x0, blocking collectives: 13.6 us -> none  [on_device_gather(): mine = lax.all_to_all(table, 'ep', split_axis=0, concat_axis=0, tiled=True)]
    unnamed x24 -> x41, local copies, waits for them, and re-layouts: 2.13 us -> 6.3 us
    dot_general x1, matrix products: 4.91 us -> 1.37 us  [on_device_gather(): jnp.einsum('bst,btd->bsd', pick, cot_all, preferred_element_type=f32)]
    all_to_all x1 -> x0, starting transfers between devices: 3.47 us -> none  [on_device_gather(): lax.all_to_all(route_rows, 'ep', split_axis=0, concat_axis=0, tiled=True)]
  transfers between devices with their start and end apart: 5 -> 0, of which waited for: 4 -> 0; matrix products, arithmetic and copies ran while one was open for 12% -> 0% of each run, Pallas kernels for 0% -> 0%
where the time goes in v2:
time: 288 us
  Pallas kernels  182 us (63%)
  blocking collectives  38.6 us (13%)
  matrix products  35.1 us (12%)
  other arithmetic  18.3 us (6%)
  local copies, waits for them, and re-layouts  11.9 us (4%)
    pallas_call x1, Pallas kernels, gather_blocks(): pl.pallas_call(functools.partial(gather_kernel, groups), out_shape=[jax.S...  123 us
    pallas_call x1, Pallas kernels, combine(): pl.pallas_call(functools.partial(combine_kernel, groups), out_shape=[jax....  59.7 us
    psum x1, blocking collectives, finish(): square_sum = lax.psum(jnp.sum(grad_share * grad_share), ('dp', 'ep'))  38.6 us
    convert_element_type x1, other arithmetic, finish(): update.astype(jnp.bfloat16)  8.35 us
    unnamed x41, local copies, waits for them, and re-layouts  6.3 us

profile of v2, /device:TPU:0, one launch (start us, length us, event | category | flops | bytes accessed | tf_op | source)
XLA Modules:
  0.0 287.8 jit_solution(16262030562258345158)
XLA Ops:
  0.6 0.5 iota_compare_fusion.2
  1.2 0.7 convert_element_type.98
  1.8 0.7 select_reduce_fusion.1
  2.5 0.0 copy-start
  2.6 1.0 copy-done
  3.6 1.0 copy-done.1
  4.6 122.6 %shard_map.110 = (bf16[16,128,2048]{2,1,0:T(8,128)(2,1)}, bf16[16,128,2048]{2,1,0:T(8,128)(2,1)}, bf16[16,16,128]{2,1,0:T(8,128)(2,1)S(1)}) custom-call(bf16[128,2048]{1,0:T(8,128)(2,1)S(1)} %copy-done, bf16[128,2048]{1,0:T(8,128)(2,1)S(1)} %copy-done.1, bf16[16,128]{1,0:T(8,128)(2,1)S(1)} %bitcast.68), custom_call_target="tpu_custom_call" | custom-call | tf_op jit(solution)/shard_map/pallas_call | solution.py:289
  127.2 0.6 dynamic-slice_convert_fusion.3
  127.9 0.3 reduce_window_sum.17
  128.2 4.9 %convolution_convert_fusion.1 = bf16[16,72,2048]{2,1,0:T(8,128)(2,1)S(1)} fusion(bf16[16,128,2048]{2,1,0:T(8,128)(2,1)} %get-tuple-element.13, s32[16,128]{1,0:T(8,128)S(1)} %broadcast_add_fusion, pred[16,128]{1,0:T(8,128)(4,1)S(1)} %get-tuple-element.20), kind=kOutput, calls=%fused_computation.13 | convolution fusion | flops 606633984 | bytes 13117440 | tf_op jit(solution)/shard_map/bst,btd->bsd/dot_general | solution.py:502
  133.1 0.9 copy-done.2
  133.9 1.4 convolution_convert_fusion.2
  135.3 0.2 slice-done.2
  135.6 0.6 slice-done.3
  136.1 2.4 fusion.10
  138.5 2.5 multiply_convert_fusion.2
  141.0 0.0 copy-start.12
  141.1 0.0 copy-done.4
  141.1 3.6 %multiply_reduce_fusion.1 = (bf16[1152]{0:T(1024)(128)(2,1)S(1)}, f32[1152,384]{0,1:T(8,128)}) fusion(bf16[1152,384]{0,1:T(8,128)(2,1)S(1)} %get-tuple-element.26, bf16[1152,2048]{1,0:T(8,128)(2,1)S(1)} %bitcast.76, bf16[1,3,2048,384]{3,2,1,0:T(8,128)(2,1)S(1)} %bitcast.79), kind=kOutput, calls=%fused_computation.18 | convolution fusion | flops 1813265280 | bytes 8947968 | tf_op jit(solution)/shard_map/dot_general | solution.py:514
  144.7 0.0 copy-done.12
  144.7 0.7 reshape.57
  145.4 1.8 fusion.26
  147.2 1.4 mul.122
  148.6 2.5 multiply_convert_fusion.3
  151.1 0.4 copy-done.5
  151.5 0.3 copy-done.13
  151.8 3.3 %fusion.3 = f32[2048,384]{1,0:T(8,128)S(1)} fusion(bf16[1152,384]{0,1:T(8,128)(2,1)S(1)} %copy-done.13, bf16[1152,2048]{1,0:T(8,128)(2,1)S(1)} %bitcast.77, f32[1152]{0:T(1024)S(1)} %copy-done.9), kind=kOutput, calls=%fused_computation.7 | convolution fusion | flops 1819017216 | bytes 8753664 | tf_op jit(solution)/shard_map/dot_general | solution.py:524
  155.0 0.1 select_convert_fusion.rt
  155.1 0.1 fusion.24
  155.2 2.8 fusion.40
  158.1 2.8 fusion.39
  160.9 1.9 dynamic-slice_bitcast_fusion
  162.8 0.2 fusion.22
  163.0 0.0 slice-start.5
  163.0 1.3 dynamic-slice_bitcast_fusion.2
  164.3 0.3 pad_maximum_fusion.g_ref
  164.6 0.9 slice-done.4
  165.6 0.1 slice-done.5
  165.7 2.8 fusion.8
  168.6 2.9 %fusion = bf16[1152,2048]{1,0:T(8,128)(2,1)S(1)} fusion(f32[1152,2048]{1,0:T(8,128)S(1)} %fusion.8, bf16[1152,384]{0,1:T(8,128)(2,1)S(1)} %get-tuple-element.24, bf16[1,3,2048,384]{3,2,1,0:T(8,128)(2,1)S(1)} %bitcast.81), kind=kOutput, calls=%fused_computation.2 | convolution fusion | flops 1816657920 | bytes 16613376 | tf_op jit(solution)/shard_map/dot_general | solution.py:532
  171.5 5.6 %convolution_convert_fusion.sp = bf16[16,128,2048]{2,1,0:T(8,128)(2,1)} fusion(bf16[16,72,2048]{2,1,0:T(8,128)(2,1)S(1)} %bitcast.69, s32[16,128]{1,0:T(8,128)S(1)} %broadcast_add_fusion, pred[16,128]{1,0:T(8,128)(4,1)S(1)} %get-tuple-element.20), kind=kOutput, calls=%fused_computation.4 | convolution fusion | flops 608468992 | bytes 13117440 | tf_op jit(solution)/shard_map/bst,bsd->btd/dot_general | solution.py:534
  177.2 59.7 %shard_map.111 = (bf16[128,2048]{1,0:T(8,128)(2,1)S(1)}, bf16[16,128]{1,0:T(8,128)(2,1)S(1)}, bf16[3,1024,384]{2,1,0:T(8,128)(2,1)S(1)}) custom-call(bf16[16,128,2048]{2,1,0:T(8,128)(2,1)} %convolution_convert_fusion.sp, bf16[16,16,128]{2,1,0:T(8,128)(2,1)S(1)} %select_convert_fusion.rt, bf16[3,1024,384]{2,1,0:T(8,128)(2,1)S(1)} %pad_maximum_fusion.g_ref), custom_call_target="tpu_custom_call" | custom-call | tf_op jit(solution)/shard_map/pallas_call | solution.py:460
  236.9 0.0 copy-start.10
  236.9 1.8 multiply_reduce_fusion
  238.7 38.6 %psum.7 = f32[]{:T(128)} all-reduce(f32[]{:T(128)} %multiply_reduce_fusion), channel_id=1, replica_groups=mesh['dp'=2,'ep'=16] {'dp','ep'}, use_global_device_ids=true, to_apply=%region_7.8 | all-reduce | flops 1 | bytes 8 | tf_op jit(solution)/shard_map/psum | solution.py:110
  278.0 0.6 select_reduce_fusion
  278.6 8.4 %divide_convert_fusion = (bf16[1,3,1024,384]{3,2,1,0:T(8,128)(2,1)}, bf16[1,3,1024,384]{3,2,1,0:T(8,128)(2,1)}, bf16[1,3,1024,384]{3,2,1,0:T(8,128)(2,1)}) fusion(bf16[1,3,1024,384]{3,2,1,0:T(8,128)(2,1)} %param.12, bf16[1,3,1024,384]{3,2,1,0:T(8,128)(2,1)} %param.13, f32[]{:T(128)S(6)} %min.3, bf16[3,1024,384]{2,1,0:T(8,128)(2,1)S(1)} %get-tuple-element.16, ...), kind=kLoop, calls=%fused_computation.10 | loop fusion | flops 24772608 | bytes 18874372 | tf_op jit(solution)/shard_map/convert_element_type | solution.py:124
  287.0 0.8 copy.39
  (32 shorter events, 0.1 us)
Async XLA Ops:
  2.5 1.0 copy-start
  3.6 1.0 copy-start.1
  128.2 5.8 %copy-start.2 = (bf16[16,128,2048]{2,1,0:T(8,128)(2,1)S(1)}, bf16[16,128,2048]{2,1,0:T(8,128)(2,1)}, u32[]{:S(2)}) copy-start(bf16[16,128,2048]{2,1,0:T(8,128)(2,1)} %get-tuple-element.12) | copy-start | bytes 25165828
  128.2 7.4 %slice-start.2 = ((s8[4718592]{0:T(1024)(128)(4,1)}), s8[4194304]{0:T(1024)(128)(4,1)S(1)}, s32[]{:S(2)}) async-start(s8[4718592]{0:T(1024)(128)(4,1)} %bitcast.78), calls=%async_computation.2 | async-start | bytes 8388608
  133.9 4.6 %copy-start.3 = (bf16[16,72,2048]{2,1,0:T(8,128)(2,1)}, bf16[16,72,2048]{2,1,0:T(8,128)(2,1)S(1)}, u32[]{:S(2)}) copy-start(bf16[16,72,2048]{2,1,0:T(8,128)(2,1)S(1)} %convolution_convert_fusion.1) | copy-start | bytes 14155780
  133.9 2.2 slice-start.3
  135.3 5.7 %copy-start.4 = (bf16[16,72,2048]{2,1,0:T(8,128)(2,1)}, bf16[16,72,2048]{2,1,0:T(8,128)(2,1)S(1)}, u32[]{:S(2)}) copy-start(bf16[16,72,2048]{2,1,0:T(8,128)(2,1)S(1)} %convolution_convert_fusion.2) | copy-start | bytes 14155780
  141.0 3.6 %copy-start.12 = (bf16[1152,384]{0,1:T(8,128)(2,1)}, bf16[1152,384]{0,1:T(8,128)(2,1)S(1)}, u32[]{:S(2)}) copy-start(bf16[1152,384]{0,1:T(8,128)(2,1)S(1)} %get-tuple-element.26) | copy-start | bytes 2654212
  148.6 2.9 %copy-start.5 = (bf16[16,72,2048]{2,1,0:T(8,128)(2,1)S(1)}, bf16[16,72,2048]{2,1,0:T(8,128)(2,1)}, u32[]{:S(2)}) copy-start(bf16[16,72,2048]{2,1,0:T(8,128)(2,1)} %copy-done.4) | copy-start | bytes 14155780
  148.6 2.9 %copy-start.9 = (f32[1152]{0:T(1024)S(1)}, f32[1152]{0:T(1024)}, u32[]{:S(2)}) copy-start(f32[1152]{0:T(1024)} %mul.122) | copy-start | bytes 13828
  148.6 3.1 %copy-start.13 = (bf16[1152,384]{0,1:T(8,128)(2,1)S(1)}, bf16[1152,384]{0,1:T(8,128)(2,1)}, u32[]{:S(2)}) copy-start(bf16[1152,384]{0,1:T(8,128)(2,1)} %copy-done.12) | copy-start | bytes 2654212
  148.6 6.6 %slice-start = ((s8[4718592]{0:T(1024)(128)(4,1)}), s8[524288]{0:T(1024)(128)(4,1)S(1)}, s32[]{:S(2)}) async-start(s8[4718592]{0:T(1024)(128)(4,1)} %bitcast.72), calls=%async_computation | async-start | bytes 1048576
  151.7 3.3 %copy-start.11 = (pred[16]{0:T(512)(128)(4,1)S(1)}, pred[16]{0:T(512)(128)(4,1)}, u32[]{:S(2)}) copy-start(pred[16]{0:T(512)(128)(4,1)} %iota_compare_fusion.2) | copy-start | bytes 52
  151.8 3.5 %slice-start.1 = ((s8[4718592]{0:T(1024)(128)(4,1)}), s8[4194304]{0:T(1024)(128)(4,1)S(1)}, s32[]{:S(2)}) async-start(s8[4718592]{0:T(1024)(128)(4,1)} %bitcast.72), calls=%async_computation.1 | async-start | bytes 8388608
  162.8 2.8 slice-start.4
  163.0 2.7 slice-start.5
  177.1 59.7 %copy-start.6 = (f32[1,1024,384]{2,1,0:T(8,128)S(1)}, f32[1,1024,384]{2,1,0:T(8,128)}, u32[]{:S(2)}) copy-start(f32[1,1024,384]{2,1,0:T(8,128)} %get-tuple-element.32) | copy-start | bytes 4718596
  177.1 59.7 %copy-start.7 = (f32[1,1024,384]{2,1,0:T(8,128)S(1)}, f32[1,1024,384]{2,1,0:T(8,128)}, u32[]{:S(2)}) copy-start(f32[1,1024,384]{2,1,0:T(8,128)} %get-tuple-element.33) | copy-start | bytes 4718596
  177.2 59.7 %copy-start.8 = (f32[1,1024,384]{2,1,0:T(8,128)S(1)}, f32[1,1024,384]{2,1,0:T(8,128)}, u32[]{:S(2)}) copy-start(f32[1,1024,384]{2,1,0:T(8,128)} %dynamic-slice_bitcast_fusion.2) | copy-start | bytes 4718596
  236.9 41.2 %copy-start.10 = (s32[128,8]{0,1:T(8,128)S(1)}, s32[128,8]{0,1:T(8,128)}, u32[]{:S(2)}) copy-start(s32[128,8]{0,1:T(8,128)} %param.9) | copy-start | bytes 12292

commit v3 on v2

--- a/solution.py
+++ b/solution.py
@@ -106,8 +106,7 @@
     )
 
 
-def finish(grad_share, first_moment, second_moment, param_count):
-    square_sum = lax.psum(jnp.sum(grad_share * grad_share), ("dp", "ep"))
+def finish(grad_share, square_sum, first_moment, second_moment, param_count):
     root_mean = jnp.sqrt(square_sum / param_count + 1e-06)
     clip_factor = jnp.minimum(1.0, 0.5 / root_mean)
     clipped = clip_factor * grad_share
@@ -153,17 +152,12 @@
         hello(partner)
         expected = 3
 
-    @pl.when(z > 0)
-    def _():
-        hello({"ep": index_of(z - 1, y, core)})
-
-    @pl.when(z < depth - 1)
-    def _():
-        hello({"ep": index_of(z + 1, y, core)})
-
-    pl.semaphore_wait(
-        barrier, expected + jnp.where(z > 0, 1, 0) + jnp.where(z < depth - 1, 1, 0)
-    )
+    for level in range(depth):
+        @pl.when(z != level)
+        def _():
+            hello({"ep": index_of(level, y, core)})
+
+    pl.semaphore_wait(barrier, expected + depth - 1)
 
 
 def gather_kernel(groups, x_ref, c_ref, t_ref, xs, cs, ts, up_sem, down_sem, y_sem, core_sem, recv_sem, own_sem):
@@ -172,100 +166,101 @@
     arrays = ((x_ref, xs), (c_ref, cs), (t_ref, ts))
     greet(z, y, core, depth, None)
 
-    def copies(block, source_own, sems, slot, device):
-        return [
-            pltpu.make_async_remote_copy(
-                src_ref=own if source_own else full.at[block],
-                dst_ref=full.at[block],
-                send_sem=sems.at[i, slot],
-                recv_sem=recv_sem.at[i, block],
-                device_id={"ep": device},
-                device_id_type=MESH,
-            )
-            for i, (own, full) in enumerate(arrays)
-        ]
-
-    def start(block, source_own, sems, slot, device):
-        for copy in copies(block, source_own, sems, slot, device):
-            copy.start()
-
-    def arrived(block):
-        for copy in copies(block, False, core_sem, 0, index_of(z, y, 1 - core)):
-            copy.wait_recv()
+    above, below = index_of(z + 1, y, core), index_of(z - 1, y, core)
+    beside, sibling = index_of(z, 1 - y, core), index_of(z, y, 1 - core)
+    paired = z + 1 - 2 * lax.rem(z, 2)
+
+    def copy(i, block, source_own, sems, slot, device):
+        own, full = arrays[i]
+        return pltpu.make_async_remote_copy(
+            src_ref=own if source_own else full.at[block],
+            dst_ref=full.at[block],
+            send_sem=sems.at[i, slot],
+            recv_sem=recv_sem.at[i, block],
+            device_id={"ep": device},
+            device_id_type=MESH,
+        )
+
+    def arrived(i, block):
+        copy(i, block, False, core_sem, 0, sibling).wait_recv()
 
     local = [
         pltpu.make_async_copy(own, full.at[me], own_sem.at[i])
         for i, (own, full) in enumerate(arrays)
     ]
-    above, below = index_of(z + 1, y, core), index_of(z - 1, y, core)
-    beside, sibling = index_of(z, 1 - y, core), index_of(z, y, 1 - core)
-
-    @pl.when(z < depth - 1)
-    def _():
-        start(me, True, up_sem, z, above)
-
-    @pl.when(z > 0)
-    def _():
-        start(me, True, down_sem, z, below)
-
-    start(me, True, y_sem, z, beside)
-    start(me, True, core_sem, z * 2 + y, sibling)
-    for copy in local:
-        copy.start()
-
-    def pass_on(level, side):
-        block = index_of(level, side, core)
-        arrived(block)
-        start(block, False, core_sem, level * 2 + side, sibling)
-        return block
+    for i in range(3):
+        @pl.when(z < depth - 1)
+        def _():
+            copy(i, me, True, up_sem, z, above).start()
+
+        @pl.when(z > 0)
+        def _():
+            copy(i, me, True, down_sem, z, below).start()
+
+        copy(i, me, True, y_sem, z, beside).start()
+        copy(i, me, True, core_sem, z * 2 + y, sibling).start()
+    for each in local:
+        each.start()
+
+    def spread_column(i, level, onward, sems, device):
+        block = index_of(level, y, core)
+        arrived(i, block)
+
+        @pl.when(onward)
+        def _():
+            copy(i, block, False, sems, level, device).start()
+
+        if i == 1:
+            @pl.when(level != paired)
+            def _():
+                copy(i, block, False, y_sem, level, beside).start()
+        else:
+            copy(i, block, False, y_sem, level, beside).start()
+        copy(i, block, False, core_sem, level * 2 + y, sibling).start()
+
+    for step in range(1, depth):
+        for i in range(3):
+            @pl.when(z - step >= 0)
+            def _():
+                spread_column(i, z - step, z < depth - 1, up_sem, above)
+
+            @pl.when(z + step <= depth - 1)
+            def _():
+                spread_column(i, z + step, z > 0, down_sem, below)
+
+        if step == 1:
+            far = index_of(z, 1 - y, core)
+            for i in range(3):
+                arrived(i, far)
+                if i == 1:
+                    copy(i, far, False, y_sem, paired, index_of(paired, y, core)).start()
+                copy(i, far, False, core_sem, z * 2 + 1 - y, sibling).start()
+
+    def pass_on(level):
+        far = index_of(level, 1 - y, core)
+        for i in range(3):
+            arrived(i, far)
+            copy(i, far, False, core_sem, level * 2 + 1 - y, sibling).start()
 
     for step in range(1, depth):
         @pl.when(z - step >= 0)
         def _():
-            level = z - step
-            block = index_of(level, y, core)
-            arrived(block)
-
-            @pl.when(z < depth - 1)
-            def _():
-                start(block, False, up_sem, level, above)
-
-            start(block, False, y_sem, level, beside)
-            start(block, False, core_sem, level * 2 + y, sibling)
+            pass_on(z - step)
 
         @pl.when(z + step <= depth - 1)
         def _():
-            level = z + step
-            block = index_of(level, y, core)
-            arrived(block)
-
-            @pl.when(z > 0)
-            def _():
-                start(block, False, down_sem, level, below)
-
-            start(block, False, y_sem, level, beside)
-            start(block, False, core_sem, level * 2 + y, sibling)
-
-        if step == 1:
-            pass_on(z, 1 - y)
-
-        @pl.when(z - step >= 0)
-        def _():
-            pass_on(z - step, 1 - y)
-
-        @pl.when(z + step <= depth - 1)
-        def _():
-            pass_on(z + step, 1 - y)
+            pass_on(z + step)
 
     for level in range(depth):
         for side in range(2):
-            arrived(index_of(level, side, 1 - core))
-    for copy in local:
-        copy.wait()
+            for i in range(3):
+                arrived(i, index_of(level, side, 1 - core))
+    for each in local:
+        each.wait()
 
     def sent(sems, slot, device):
-        for copy in copies(me, True, sems, slot, device):
-            copy.wait_send()
+        for i in range(3):
+            copy(i, me, True, sems, slot, device).wait_send()
 
     for level in range(depth):
         @pl.when((z < depth - 1) & (level <= z))
@@ -306,9 +301,9 @@
 
 
 def combine_kernel(
-    groups, sp, rt, g_ref, out, route_out, g_got,
+    groups, sp, rt, g_ref, kept, out, route_out, g_got, squares,
     core_s, core_r, ys_s, ys_r, y_s, y_r, zs_s, zs_r, in_s, in_r,
-    core_send, core_recv, y_send, y_recv, z_send, z_recv, g_sem,
+    core_send, core_recv, y_send, y_recv, z_send, z_recv, g_sem, n_out, n_in, n_send, n_recv,
 ):
     z, y, core, depth = place(groups)
     partner = {"dp": 1 - lax.axis_index("dp")}
@@ -446,8 +441,48 @@
             each(z_copy(t, beside, t), "wait_send")
     g_copy.wait()
 
-
-def combine(spread, routes, sent, groups):
+    units, width, piece = kept.shape[0], kept.shape[2], 32
+
+    def square(i, carry):
+        rows = pl.ds(pl.multiple_of(i * piece, piece), piece)
+        for unit in range(units):
+            share = kept[unit, rows, :] + g_got[unit, rows, :].astype(f32)
+            carry = carry + share * share
+        return carry
+
+    sums = lax.fori_loop(0, kept.shape[1] // piece, square, jnp.zeros((piece, width), f32))
+    sums = sum(sums[i * 8:(i + 1) * 8] for i in range(piece // 8))
+    sums = sum(sums[:, i * 128:(i + 1) * 128] for i in range(width // 128))
+
+    def share_sum(src, dst, device, recv):
+        return pltpu.make_async_remote_copy(
+            src_ref=n_out.at[src], dst_ref=n_in.at[dst], send_sem=n_send.at[recv],
+            recv_sem=n_recv.at[dst], device_id=device, device_id_type=MESH,
+        )
+
+    for stage, device in enumerate(
+        (partner, {"ep": index_of(z, y, 1 - core)}, {"ep": index_of(z, 1 - y, core)})
+    ):
+        n_out[stage] = sums
+        trade = share_sum(stage, stage, device, stage)
+        trade.start()
+        trade.wait()
+        sums = sums + n_in[stage]
+    n_out[3] = sums
+    for level in range(depth):
+        @pl.when(z != level)
+        def _():
+            share_sum(3, 3 + z, {"ep": index_of(level, y, core)}, 3 + level).start()
+
+    squares[...] = sums
+    for level in range(depth):
+        @pl.when(z != level)
+        def _():
+            share_sum(3, 3 + level, {"ep": index_of(level, y, core)}, 3 + level).wait()
+            squares[...] += n_in[3 + level]
+
+
+def combine(spread, routes, sent, kept, groups):
     depth = groups // 4
     bf16 = jnp.bfloat16
     big, small = spread.shape[1:], routes.shape[1:]
@@ -463,20 +498,25 @@
             jax.ShapeDtypeStruct(big, bf16),
             jax.ShapeDtypeStruct(small, bf16),
             jax.ShapeDtypeStruct(sent.shape, bf16),
+            jax.ShapeDtypeStruct((8, 128), jnp.float32),
         ],
-        in_specs=[vmem, vmem, any_space],
-        out_specs=[vmem, vmem, any_space],
+        in_specs=[vmem, vmem, any_space, vmem],
+        out_specs=[vmem, vmem, vmem, vmem],
         scratch_shapes=both(2 * depth) + both(depth) + both(depth) + both(depth) + both(2 * depth)
         + [
             dma((2, 2 * depth)), dma((2, 2 * depth)),
             dma((2, depth)), dma((2, depth)),
             dma((2, depth)), dma((2, 2 * depth)),
             dma((2,)),
+            pltpu.VMEM((4, 8, 128), jnp.float32),
+            pltpu.VMEM((3 + depth, 8, 128), jnp.float32),
+            dma((3 + depth,)),
+            dma((3 + depth,)),
         ],
         compiler_params=pltpu.CompilerParams(
-            collective_id=2, has_side_effects=True, vmem_limit_bytes=48 * MIB
+            collective_id=2, has_side_effects=True, vmem_limit_bytes=52 * MIB
         ),
-    )(spread, routes, sent)
+    )(spread, routes, sent, kept)
 
 
 def on_device_gather(
@@ -518,15 +558,19 @@
     dup = (scaled * activated).astype(bf16)
     down_cot = (row_weight * recv_cot.astype(f32)).astype(bf16)
     by_row = (((0,), (0,)), ((), ()))
-    grads = [
-        lax.dot_general(recv_x, dgate, by_row, preferred_element_type=f32),
-        lax.dot_general(recv_x, dup, by_row, preferred_element_type=f32),
-        lax.dot_general(down_cot, hidden, by_row, preferred_element_type=f32),
-    ]
     half = model_width // 2
     part = lax.axis_index("dp")
-    kept = jnp.stack([lax.dynamic_slice_in_dim(g, part * half, half, 0) for g in grads])
-    sent = jnp.stack([lax.dynamic_slice_in_dim(g, (1 - part) * half, half, 0) for g in grads])
+
+    def grads(owner, kind):
+        columns = lambda a: lax.dynamic_slice_in_dim(a, owner * half, half, 1)
+        return jnp.stack(
+            [
+                lax.dot_general(columns(rows_of), by, by_row, preferred_element_type=f32).astype(kind)
+                for rows_of, by in ((recv_x, dgate), (recv_x, dup), (down_cot, hidden))
+            ]
+        )
+
+    sent, kept = grads(1 - part, bf16), grads(part, f32)
     by_col = (((1,), (1,)), ((), ()))
     slot_back = lax.dot_general(dgate, w_gate, by_col, preferred_element_type=f32)
     slot_back = slot_back + lax.dot_general(dup, w_up, by_col, preferred_element_type=f32)
@@ -537,13 +581,17 @@
     )
     my_row = jnp.arange(experts, dtype=jnp.int32)[None, :, None] == me
     routes = jnp.where(my_row, route_rows[:, None, :], 0.0).astype(bf16)
-    token_grad, route_back, got = combine(spread, routes, sent.astype(bf16), groups)
+    token_grad, route_back, got, squares = combine(spread, routes, sent, kept, groups)
     routing_grad = jnp.sum(
         jnp.where(named, route_back.T.astype(f32)[:, None, :], 0.0), 2
     ).astype(bf16)
     grad_share = (kept + got.astype(f32))[None]
     return (token_grad, routing_grad) + finish(
-        grad_share, first_moment, second_moment, 3.0 * experts * model_width * hidden_units
+        grad_share,
+        jnp.sum(squares),
+        first_moment,
+        second_moment,
+        3.0 * experts * model_width * hidden_units,
     )
 
 

time: 288 us -> 250 us (0.87)
  blocking collectives: 38.6 us -> 0 us
  matrix products: 35.1 us -> 46.9 us
  Pallas kernels: 182 us -> 173 us
  local copies, waits for them, and re-layouts: 11.9 us -> 3.11 us
  other arithmetic: 18.3 us -> 24.4 us
    psum x1 -> x0, blocking collectives: 38.6 us -> none  [finish(): square_sum = lax.psum(jnp.sum(grad_share * grad_share), ('dp', 'ep'))]
    pallas_call x1, Pallas kernels: 123 us -> 101 us  [gather_blocks(): pl.pallas_call(functools.partial(gather_kernel, groups), out_shape=[jax.S...]
    pallas_call x1, Pallas kernels: 59.7 us -> 72.5 us  [combine(): pl.pallas_call(functools.partial(combine_kernel, groups), out_shape=[jax....]
    dot_general x3 -> x6, matrix products: 8.89 us -> 16.4 us  [grads(): lax.dot_general(columns(rows_of), by, by_row, preferred_element_type=f32)]
    another operation x1 -> x2, other arithmetic: 0.31 us -> 5.64 us  [grads(): jnp.stack([lax.dot_general(columns(rows_of), by, by_row, preferred_elemen...]
    another operation x4 -> x0, local copies, waits for them, and re-layouts: 3.51 us -> none  [the longest x2 3.25 us: on_device_gather(): jnp.stack([lax.dynamic_slice_in_dim(g, part * half, half, 0) for g in gra...]
    unnamed x41 -> x39, local copies, waits for them, and re-layouts: 6.3 us -> 2.95 us
    convert_element_type x0 -> x1, other arithmetic: none -> 3.03 us  [on_device_gather(): down_cot = (row_weight * recv_cot.astype(f32)).astype(bf16)]
where the time goes in v3:
time: 250 us; the launch traced here: 249 us
  Pallas kernels  173 us (69%)
  matrix products  46.9 us (19%)
  other arithmetic  24.4 us (10%)
  local copies, waits for them, and re-layouts  3.11 us (1%)
    pallas_call x1, Pallas kernels, gather_blocks(): pl.pallas_call(functools.partial(gather_kernel, groups), out_shape=[jax.S...  101 us
    pallas_call x1, Pallas kernels, combine(): pl.pallas_call(functools.partial(combine_kernel, groups), out_shape=[jax....  72.5 us
    dot_general x6, matrix products, grads(): lax.dot_general(columns(rows_of), by, by_row, preferred_element_type=f32)  16.4 us
    convert_element_type x1, other arithmetic, finish(): update.astype(jnp.bfloat16)  8.51 us
    dot_general x1, matrix products, on_device_gather(): jnp.einsum('bst,bsd->btd', pick, slot_back, preferred_element_type=f32)  5.66 us
    another operation x2, other arithmetic, grads(): jnp.stack([lax.dot_general(columns(rows_of), by, by_row, preferred_elemen...  5.64 us

profile of v3, /device:TPU:0, one launch (start us, length us, event | category | flops | bytes accessed | tf_op | source)
XLA Modules:
  0.0 249.2 jit_solution(11829712876544450687)
XLA Ops:
  0.6 0.7 convert_element_type.106
  1.3 0.7 select_reduce_fusion.1
  2.0 0.0 copy-start
  2.0 1.0 copy-done
  3.1 1.0 copy-done.1
  4.1 100.7 %shard_map.110 = (bf16[16,128,2048]{2,1,0:T(8,128)(2,1)}, bf16[16,128,2048]{2,1,0:T(8,128)(2,1)}, bf16[16,16,128]{2,1,0:T(8,128)(2,1)S(1)}) custom-call(bf16[128,2048]{1,0:T(8,128)(2,1)S(1)} %copy-done, bf16[128,2048]{1,0:T(8,128)(2,1)S(1)} %copy-done.1, bf16[16,128]{1,0:T(8,128)(2,1)S(1)} %bitcast.70), custom_call_target="tpu_custom_call" | custom-call | tf_op jit(solution)/shard_map/pallas_call | solution.py:284
  104.9 0.3 reduce_window_sum.17
  105.2 4.9 %convolution_convert_fusion.1 = bf16[16,72,2048]{2,1,0:T(8,128)(2,1)S(1)} fusion(bf16[16,128,2048]{2,1,0:T(8,128)(2,1)} %get-tuple-element.14, s32[16,128]{1,0:T(8,128)S(1)} %broadcast_add_fusion, pred[16,128]{1,0:T(8,128)(4,1)S(1)} %get-tuple-element.22), kind=kOutput, calls=%fused_computation.11 | convolution fusion | flops 606633984 | bytes 13117440 | tf_op jit(solution)/shard_map/bst,btd->bsd/dot_general | solution.py:542
  110.1 0.0 copy-start.3
  110.1 0.0 slice-done.8
  110.1 0.0 slice-done.9
  110.2 0.0 slice-start.2
  110.2 2.4 fusion.18
  112.6 0.0 copy-done.3
  112.6 0.0 copy-start.6
  112.6 0.0 slice-start.3
  112.6 3.8 %multiply_convert_fusion.1 = (bf16[1152,384]{0,1:T(8,128)(2,1)S(1)}, f32[1152,384]{0,1:T(8,128)}) fusion(f32[1152,384]{0,1:T(8,128)S(1)} %fusion.18, bf16[1152,2048]{1,0:T(8,128)(2,1)S(1)} %bitcast.78, bf16[1,3,2048,384]{3,2,1,0:T(8,128)(2,1)S(1)} %bitcast.88), kind=kOutput, calls=%fused_computation.27 | convolution fusion | flops 1814593536 | bytes 10715136 | tf_op jit(solution)/shard_map/dot_general | solution.py:550
  116.4 1.4 convolution_convert_fusion.2
  117.8 3.6 %multiply_reduce_fusion = (bf16[1152]{0:T(1024)(128)(2,1)S(1)}, f32[1152,384]{0,1:T(8,128)}) fusion(bf16[1152,384]{0,1:T(8,128)(2,1)S(1)} %get-tuple-element.28, bf16[1152,2048]{1,0:T(8,128)(2,1)S(1)} %bitcast.71, bf16[1,3,2048,384]{3,2,1,0:T(8,128)(2,1)S(1)} %bitcast.88), kind=kOutput, calls=%fused_computation.26 | convolution fusion | flops 1813265280 | bytes 8947968 | tf_op jit(solution)/shard_map/dot_general | solution.py:554
  121.4 0.1 reshape.55
  121.5 0.6 fusion.59
  122.1 0.1 mul.118
  122.2 3.6 %multiply_convert_fusion.2 = (bf16[1152,384]{0,1:T(8,128)(2,1)S(1)}, bf16[1152,384]{0,1:T(8,128)(2,1)S(1)}) fusion(f32[1152,384]{0,1:T(8,128)} %get-tuple-element.31, f32[1152]{0:T(1024)S(1)} %mul.118, f32[1152,384]{0,1:T(8,128)} %copy-done.6, f32[1152,384]{0,1:T(8,128)} %get-tuple-element.29), kind=kLoop, calls=%fused_computation.28 | loop fusion | flops 6193152 | bytes 7082496 | tf_op jit(solution)/shard_map/convert_element_type | solution.py:558
  125.8 0.0 copy-start.5
  125.8 0.0 slice-start
  125.8 4.5 %fusion.16 = f32[1152,2048]{1,0:T(8,128)S(1)} fusion(bf16[1152,384]{0,1:T(8,128)(2,1)S(1)} %get-tuple-element.27, bf16[1,3,2048,384]{3,2,1,0:T(8,128)(2,1)} %param.11), kind=kOutput, calls=%fused_computation.32 | convolution fusion | flops 1811939328 | bytes 11894784 | tf_op jit(solution)/shard_map/dot_general | solution.py:575
  130.3 0.0 slice-start.1
  130.3 4.2 %fusion = bf16[1152,2048]{1,0:T(8,128)(2,1)S(1)} fusion(f32[1152,2048]{1,0:T(8,128)S(1)} %fusion.16, bf16[1152,384]{0,1:T(8,128)(2,1)S(1)} %get-tuple-element.26, bf16[1,3,2048,384]{3,2,1,0:T(8,128)(2,1)} %param.11), kind=kOutput, calls=%fused_computation.2 | convolution fusion | flops 1816657920 | bytes 16613376 | tf_op jit(solution)/shard_map/dot_general | solution.py:576
  134.5 5.7 %convolution_convert_fusion.sp = bf16[16,128,2048]{2,1,0:T(8,128)(2,1)} fusion(bf16[16,72,2048]{2,1,0:T(8,128)(2,1)S(1)} %bitcast.76, s32[16,128]{1,0:T(8,128)S(1)} %broadcast_add_fusion, pred[16,128]{1,0:T(8,128)(4,1)S(1)} %get-tuple-element.22), kind=kOutput, calls=%fused_computation.4 | convolution fusion | flops 608468992 | bytes 13117440 | tf_op jit(solution)/shard_map/bst,bsd->btd/dot_general | solution.py:578
  140.2 0.1 select_convert_fusion.rt
  140.3 0.0 slice-done
  140.3 0.0 slice-done.1
  140.3 3.0 %multiply_convert_fusion = bf16[1152,2048]{1,0:T(8,128)(2,1)} fusion(f32[1152]{0:T(1024)S(1)} %mul.118, bf16[16,72,2048]{2,1,0:T(8,128)(2,1)S(1)} %bitcast.73), kind=kLoop, calls=%fused_computation.1 | loop fusion | flops 7077888 | bytes 9441792 | tf_op jit(solution)/shard_map/convert_element_type | solution.py:559
  143.3 3.5 %fusion.48 = bf16[1,1024,384]{2,1,0:T(8,128)(2,1)S(1)} fusion(bf16[1152,384]{0,1:T(8,128)(2,1)} %copy-done.8, bf16[1152,2048]{1,0:T(8,128)(2,1)} %multiply_convert_fusion, s32[]{:T(128)S(6)} %select_n.28), kind=kOutput, calls=%fused_computation.52 | convolution fusion | flops 906362880 | bytes 4030468 | tf_op jit(solution)/shard_map/dot_general | solution.py:568
  146.9 1.5 fusion.51
  148.5 1.8 fusion.54
  150.2 0.0 slice-start.6
  150.3 1.7 pad_maximum_fusion.1.g_ref
  152.0 3.5 %fusion.32 = f32[1,1024,384]{2,1,0:T(8,128)S(1)} fusion(bf16[1152,384]{0,1:T(8,128)(2,1)} %copy-done.8, bf16[1152,2048]{1,0:T(8,128)(2,1)} %multiply_convert_fusion, s32[]{:T(128)S(6)} %select_n.29), kind=kOutput, calls=%fused_computation.44 | convolution fusion | flops 905969664 | bytes 4816900 | tf_op jit(solution)/shard_map/dot_general | solution.py:568
  155.5 3.4 %fusion.29 = f32[1,1024,384]{2,1,0:T(8,128)S(1)} fusion(bf16[1152,384]{0,1:T(8,128)(2,1)} %copy-done.5, bf16[1152,2048]{1,0:T(8,128)(2,1)} %bitcast.79, s32[]{:T(128)S(6)} %select_n.29), kind=kOutput, calls=%fused_computation.43 | convolution fusion | flops 905969664 | bytes 4816900 | tf_op jit(solution)/shard_map/dot_general | solution.py:568
  158.9 0.0 copy-start.4
  158.9 2.7 %fusion.26 = f32[1,1024,384]{2,1,0:T(8,128)} fusion(bf16[1152,384]{0,1:T(8,128)(2,1)S(1)} %get-tuple-element.27, bf16[1152,2048]{1,0:T(8,128)(2,1)S(1)} %bitcast.86, s32[]{:T(128)S(6)} %select_n.29), kind=kOutput, calls=%fused_computation.42 | convolution fusion | flops 905969664 | bytes 4816900 | tf_op jit(solution)/shard_map/dot_general | solution.py:568
  161.6 3.9 %pad_maximum_fusion.kept = f32[3,1024,384]{2,1,0:T(8,128)} fusion(f32[1,1024,384]{2,1,0:T(8,128)S(1)} %fusion.32, f32[1,1024,384]{2,1,0:T(8,128)S(1)} %fusion.29, f32[1,1024,384]{2,1,0:T(8,128)} %fusion.26), kind=kLoop, calls=%fused_computation.7 | loop fusion | flops 2359296 | bytes 9437184 | tf_op jit(solution)/shard_map/stack | solution.py:566
  165.6 72.5 %shard_map.111 = (bf16[128,2048]{1,0:T(8,128)(2,1)S(1)}, bf16[16,128]{1,0:T(8,128)(2,1)S(1)}, bf16[3,1024,384]{2,1,0:T(8,128)(2,1)}, f32[8,128]{1,0:T(8,128)S(1)}) custom-call(bf16[16,128,2048]{2,1,0:T(8,128)(2,1)} %convolution_convert_fusion.sp, bf16[16,16,128]{2,1,0:T(8,128)(2,1)S(1)} %select_convert_fusion.rt, ...), custom_call_target="tpu_custom_call" | custom-call | tf_op jit(solution)/shard_map/pallas_call | solution.py:495
  238.0 0.6 select_reduce_fusion
  238.6 0.6 reduce_sum.59
  239.9 8.5 %divide_convert_fusion = (bf16[1,3,1024,384]{3,2,1,0:T(8,128)(2,1)}, bf16[1,3,1024,384]{3,2,1,0:T(8,128)(2,1)}, bf16[1,3,1024,384]{3,2,1,0:T(8,128)(2,1)}) fusion(bf16[3,1024,384]{2,1,0:T(8,128)(2,1)} %get-tuple-element.18, f32[]{:T(128)S(6)} %min.3, bf16[1,3,1024,384]{3,2,1,0:T(8,128)(2,1)} %param.12, bf16[1,3,1024,384]{3,2,1,0:T(8,128)(2,1)} %param.13, ...), kind=kLoop, calls=%fused_computation.9 | loop fusion | flops 24772608 | bytes 18874372 | tf_op jit(solution)/shard_map/convert_element_type | solution.py:123
  248.5 0.8 copy.39
  (32 shorter events, 0.1 us)
Async XLA Ops:
  2.0 1.0 copy-start
  3.1 1.0 copy-start.1
  4.1 106.0 %slice-start.8 = ((s8[4718592]{0:T(1024)(128)(4,1)}), s8[524288]{0:T(1024)(128)(4,1)S(1)}, s32[]{:S(2)}) async-start(s8[4718592]{0:T(1024)(128)(4,1)} %bitcast.87), calls=%async_computation.8 | async-start | bytes 1048576
  105.2 4.9 %slice-start.9 = ((s8[4718592]{0:T(1024)(128)(4,1)}), s8[4194304]{0:T(1024)(128)(4,1)S(1)}, s32[]{:S(2)}) async-start(s8[4718592]{0:T(1024)(128)(4,1)} %bitcast.87), calls=%async_computation.9 | async-start | bytes 8388608
  110.1 2.4 copy-start.3
  110.2 6.2 %slice-start.2 = ((s8[8388608]{0:T(1024)(128)(4,1)}), s8[4194304]{0:T(1024)(128)(4,1)S(1)}, s32[]{:S(2)}) async-start(s8[8388608]{0:T(1024)(128)(4,1)} %bitcast.74), calls=%async_computation.2 | async-start | bytes 8388608
  112.6 3.8 %copy-start.6 = (f32[1152,384]{0,1:T(8,128)}, f32[1152,384]{0,1:T(8,128)S(1)}, u32[]{:S(2)}) copy-start(f32[1152,384]{0,1:T(8,128)S(1)} %fusion.18) | copy-start | bytes 5308420
  112.6 3.8 %slice-start.3 = ((s8[8388608]{0:T(1024)(128)(4,1)}), s8[4194304]{0:T(1024)(128)(4,1)S(1)}, s32[]{:S(2)}) async-start(s8[8388608]{0:T(1024)(128)(4,1)} %bitcast.74), calls=%async_computation.3 | async-start | bytes 8388608
  116.4 1.4 copy-start.8
  117.8 3.7 %copy-start.2 = (bf16[16,72,2048]{2,1,0:T(8,128)(2,1)}, bf16[16,72,2048]{2,1,0:T(8,128)(2,1)S(1)}, u32[]{:S(2)}) copy-start(bf16[16,72,2048]{2,1,0:T(8,128)(2,1)S(1)} %convolution_convert_fusion.2) | copy-start | bytes 14155780
  125.8 21.1 %copy-start.5 = (bf16[1152,384]{0,1:T(8,128)(2,1)}, bf16[1152,384]{0,1:T(8,128)(2,1)S(1)}, u32[]{:S(2)}) copy-start(bf16[1152,384]{0,1:T(8,128)(2,1)S(1)} %get-tuple-element.26) | copy-start | bytes 2654212
  125.8 14.5 %slice-start = ((s8[4718592]{0:T(1024)(128)(4,1)}), s8[4194304]{0:T(1024)(128)(4,1)S(1)}, s32[]{:S(2)}) async-start(s8[4718592]{0:T(1024)(128)(4,1)} %bitcast.72), calls=%async_computation | async-start | bytes 8388608
  130.3 10.0 %slice-start.1 = ((s8[4718592]{0:T(1024)(128)(4,1)}), s8[524288]{0:T(1024)(128)(4,1)S(1)}, s32[]{:S(2)}) async-start(s8[4718592]{0:T(1024)(128)(4,1)} %bitcast.72), calls=%async_computation.1 | async-start | bytes 1048576
  143.3 3.6 %slice-start.4 = ((s8[4718592]{0:T(1024)(128)(4,1)}), s8[524288]{0:T(1024)(128)(4,1)S(1)}, s32[]{:S(2)}) async-start(s8[4718592]{0:T(1024)(128)(4,1)} %bitcast.80), calls=%async_computation.4 | async-start | bytes 1048576
  143.3 3.6 %slice-start.5 = ((s8[4718592]{0:T(1024)(128)(4,1)}), s8[4194304]{0:T(1024)(128)(4,1)S(1)}, s32[]{:S(2)}) async-start(s8[4718592]{0:T(1024)(128)(4,1)} %bitcast.80), calls=%async_computation.5 | async-start | bytes 8388608
  150.2 8.7 %slice-start.6 = ((s8[4718592]{0:T(1024)(128)(4,1)}), s8[524288]{0:T(1024)(128)(4,1)S(1)}, s32[]{:S(2)}) async-start(s8[4718592]{0:T(1024)(128)(4,1)} %bitcast.84), calls=%async_computation.6 | async-start | bytes 1048576
  152.0 6.9 %slice-start.7 = ((s8[4718592]{0:T(1024)(128)(4,1)}), s8[4194304]{0:T(1024)(128)(4,1)S(1)}, s32[]{:S(2)}) async-start(s8[4718592]{0:T(1024)(128)(4,1)} %bitcast.84), calls=%async_computation.7 | async-start | bytes 8388608
  158.9 2.7 %copy-start.4 = (f32[1,1024,384]{2,1,0:T(8,128)}, f32[1,1024,384]{2,1,0:T(8,128)S(1)}, u32[]{:S(2)}) copy-start(f32[1,1024,384]{2,1,0:T(8,128)S(1)} %fusion.29) | copy-start | bytes 4718596
  165.5 72.5 %copy-start.7 = (s32[128,8]{0,1:T(8,128)S(1)}, s32[128,8]{0,1:T(8,128)}, u32[]{:S(2)}) copy-start(s32[128,8]{0,1:T(8,128)} %param.9) | copy-start | bytes 12292

commit v4 on v3

--- a/solution.py
+++ b/solution.py
@@ -301,18 +301,24 @@
 
 
 def combine_kernel(
-    groups, sp, rt, g_ref, kept, out, route_out, g_got, squares,
+    groups, sp, rt, g0, g1, g2, k0, k1, k2, out, route_out, share_out, squares,
+    g_got,
     core_s, core_r, ys_s, ys_r, y_s, y_r, zs_s, zs_r, in_s, in_r,
     core_send, core_recv, y_send, y_recv, z_send, z_recv, g_sem, n_out, n_in, n_send, n_recv,
 ):
     z, y, core, depth = place(groups)
     partner = {"dp": 1 - lax.axis_index("dp")}
     greet(z, y, core, depth, partner)
-    g_copy = pltpu.make_async_remote_copy(
-        src_ref=g_ref, dst_ref=g_got, send_sem=g_sem.at[0], recv_sem=g_sem.at[1],
-        device_id=partner, device_id_type=MESH,
-    )
-    g_copy.start()
+    g_copies = [
+        pltpu.make_async_remote_copy(
+            src_ref=g, dst_ref=g_got.at[i], send_sem=g_sem.at[0, i], recv_sem=g_sem.at[1, i],
+            device_id=partner, device_id_type=MESH,
+        )
+        for i, g in enumerate((g0, g1, g2))
+    ]
+    for copy in g_copies:
+        copy.start()
+    kept = (k0, k1, k2)
     chunk = 16
     chunks = sp.shape[1] // chunk
     f32, bf16 = jnp.float32, jnp.bfloat16
@@ -406,51 +412,20 @@
             add((zs_s, zs_r, t), terms)
 
         each(z_copy(t, going, slot), "start")
-    each(core_copy(z, y), "wait_recv")
-    each(y_copy(z), "wait_recv")
-    terms = [(sp, rt, index_of(z, y, core)), (core_s, core_r, z * 2 + y), (y_s, y_r, z)]
-    from_below, from_above = (in_s, in_r, z), (in_s, in_r, depth + z)
-    beside = jnp.where(z > 0, z - 1, z + 1)
-
-    @pl.when(z > 0)
-    def _():
-        each(z_copy(z, beside, z), "wait_recv")
-
-    @pl.when(z < depth - 1)
-    def _():
-        each(z_copy(z, beside, depth + z), "wait_recv")
-
-    @pl.when((z > 0) & (z < depth - 1))
-    def _():
-        add((out, route_out, None), terms + [from_below, from_above])
-
-    @pl.when(z == 0)
-    def _():
-        add((out, route_out, None), terms + [from_above])
-
-    @pl.when(z == depth - 1)
-    def _():
-        add((out, route_out, None), terms + [from_below])
-
-    for j in range(depth):
-        t = target(j)
-        each(core_copy(t, 0), "wait_send")
-        each(core_copy(t, 1), "wait_send")
-        each(y_copy(t), "wait_send")
-        if j < depth - 1:
-            each(z_copy(t, beside, t), "wait_send")
-    g_copy.wait()
-
-    units, width, piece = kept.shape[0], kept.shape[2], 32
+    for copy in g_copies:
+        copy.wait()
+
+    width, piece = k0.shape[1], 32
 
     def square(i, carry):
         rows = pl.ds(pl.multiple_of(i * piece, piece), piece)
-        for unit in range(units):
-            share = kept[unit, rows, :] + g_got[unit, rows, :].astype(f32)
+        for unit in range(3):
+            share = kept[unit][rows, :] + g_got[unit, rows, :].astype(f32)
+            share_out[unit, rows, :] = share
             carry = carry + share * share
         return carry
 
-    sums = lax.fori_loop(0, kept.shape[1] // piece, square, jnp.zeros((piece, width), f32))
+    sums = lax.fori_loop(0, k0.shape[0] // piece, square, jnp.zeros((piece, width), f32))
     sums = sum(sums[i * 8:(i + 1) * 8] for i in range(piece // 8))
     sums = sum(sums[:, i * 128:(i + 1) * 128] for i in range(width // 128))
 
@@ -480,6 +455,39 @@
         def _():
             share_sum(3, 3 + level, {"ep": index_of(level, y, core)}, 3 + level).wait()
             squares[...] += n_in[3 + level]
+    each(core_copy(z, y), "wait_recv")
+    each(y_copy(z), "wait_recv")
+    terms = [(sp, rt, index_of(z, y, core)), (core_s, core_r, z * 2 + y), (y_s, y_r, z)]
+    from_below, from_above = (in_s, in_r, z), (in_s, in_r, depth + z)
+    beside = jnp.where(z > 0, z - 1, z + 1)
+
+    @pl.when(z > 0)
+    def _():
+        each(z_copy(z, beside, z), "wait_recv")
+
+    @pl.when(z < depth - 1)
+    def _():
+        each(z_copy(z, beside, depth + z), "wait_recv")
+
+    @pl.when((z > 0) & (z < depth - 1))
+    def _():
+        add((out, route_out, None), terms + [from_below, from_above])
+
+    @pl.when(z == 0)
+    def _():
+        add((out, route_out, None), terms + [from_above])
+
+    @pl.when(z == depth - 1)
+    def _():
+        add((out, route_out, None), terms + [from_below])
+
+    for j in range(depth):
+        t = target(j)
+        each(core_copy(t, 0), "wait_send")
+        each(core_copy(t, 1), "wait_send")
+        each(y_copy(t), "wait_send")
+        if j < depth - 1:
+            each(z_copy(t, beside, t), "wait_send")
 
 
 def combine(spread, routes, sent, kept, groups):
@@ -497,17 +505,17 @@
         out_shape=[
             jax.ShapeDtypeStruct(big, bf16),
             jax.ShapeDtypeStruct(small, bf16),
-            jax.ShapeDtypeStruct(sent.shape, bf16),
+            jax.ShapeDtypeStruct((3,) + kept[0].shape, jnp.float32),
             jax.ShapeDtypeStruct((8, 128), jnp.float32),
         ],
-        in_specs=[vmem, vmem, any_space, vmem],
+        in_specs=[vmem] * 2 + [any_space] * 3 + [vmem] * 3,
         out_specs=[vmem, vmem, vmem, vmem],
-        scratch_shapes=both(2 * depth) + both(depth) + both(depth) + both(depth) + both(2 * depth)
+        scratch_shapes=[pltpu.VMEM((3,) + kept[0].shape, bf16)] + both(2 * depth) + both(depth) + both(depth) + both(depth) + both(2 * depth)
         + [
             dma((2, 2 * depth)), dma((2, 2 * depth)),
             dma((2, depth)), dma((2, depth)),
             dma((2, depth)), dma((2, 2 * depth)),
-            dma((2,)),
+            dma((2, 3)),
             pltpu.VMEM((4, 8, 128), jnp.float32),
             pltpu.VMEM((3 + depth, 8, 128), jnp.float32),
             dma((3 + depth,)),
@@ -516,7 +524,7 @@
         compiler_params=pltpu.CompilerParams(
             collective_id=2, has_side_effects=True, vmem_limit_bytes=52 * MIB
         ),
-    )(spread, routes, sent, kept)
+    )(spread, routes, *sent, *kept)
 
 
 def on_device_gather(
@@ -563,12 +571,10 @@
 
     def grads(owner, kind):
         columns = lambda a: lax.dynamic_slice_in_dim(a, owner * half, half, 1)
-        return jnp.stack(
-            [
-                lax.dot_general(columns(rows_of), by, by_row, preferred_element_type=f32).astype(kind)
-                for rows_of, by in ((recv_x, dgate), (recv_x, dup), (down_cot, hidden))
-            ]
-        )
+        return [
+            lax.dot_general(columns(rows_of), by, by_row, preferred_element_type=f32).astype(kind)
+            for rows_of, by in ((recv_x, dgate), (recv_x, dup), (down_cot, hidden))
+        ]
 
     sent, kept = grads(1 - part, bf16), grads(part, f32)
     by_col = (((1,), (1,)), ((), ()))
@@ -581,13 +587,12 @@
     )
     my_row = jnp.arange(experts, dtype=jnp.int32)[None, :, None] == me
     routes = jnp.where(my_row, route_rows[:, None, :], 0.0).astype(bf16)
-    token_grad, route_back, got, squares = combine(spread, routes, sent, kept, groups)
+    token_grad, route_back, share, squares = combine(spread, routes, sent, kept, groups)
     routing_grad = jnp.sum(
         jnp.where(named, route_back.T.astype(f32)[:, None, :], 0.0), 2
     ).astype(bf16)
-    grad_share = (kept + got.astype(f32))[None]
     return (token_grad, routing_grad) + finish(
-        grad_share,
+        share[None],
         jnp.sum(squares),
         first_moment,
         second_moment,

time: 250 us -> 241 us (0.964)
  matrix products: 46.9 us -> 40.6 us
  other arithmetic: 24.4 us -> 18.2 us
  local copies, waits for them, and re-layouts: 3.11 us -> 6.85 us
    another operation x2 -> x0, other arithmetic: 5.64 us -> none  [grads(): jnp.stack([lax.dot_general(columns(rows_of), by, by_row, preferred_elemen...]
    dot_general x1, matrix products: 4.91 us -> 1.37 us  [on_device_gather(): jnp.einsum('bst,btd->bsd', pick, x_all, preferred_element_type=f32)]
    dot_general x1, matrix products: 1.37 us -> 4.9 us  [on_device_gather(): jnp.einsum('bst,btd->bsd', pick, cot_all, preferred_element_type=f32)]
where the time goes in v4:
time: 241 us
  Pallas kernels  173 us (72%)
  matrix products  40.6 us (17%)
  other arithmetic  18.2 us (8%)
  local copies, waits for them, and re-layouts  6.85 us (3%)
    pallas_call x1, Pallas kernels, gather_blocks(): pl.pallas_call(functools.partial(gather_kernel, groups), out_shape=[jax.S...  101 us
    pallas_call x1, Pallas kernels, combine(): pl.pallas_call(functools.partial(combine_kernel, groups), out_shape=[jax....  72.6 us
    dot_general x6, matrix products, grads(): lax.dot_general(columns(rows_of), by, by_row, preferred_element_type=f32)  14.3 us
    convert_element_type x1, other arithmetic, finish(): update.astype(jnp.bfloat16)  7.74 us
    dot_general x1, matrix products, on_device_gather(): jnp.einsum('bst,bsd->btd', pick, slot_back, preferred_element_type=f32)  5.65 us
    dot_general x1, matrix products, on_device_gather(): jnp.einsum('bst,btd->bsd', pick, cot_all, preferred_element_type=f32)  4.9 us

profile of v4, /device:TPU:0, one launch (start us, length us, event | category | flops | bytes accessed | tf_op | source)
XLA Modules:
  0.0 240.5 jit_solution(11902315115010153590)
XLA Ops:
  0.6 0.5 iota_compare_fusion.2
  1.2 0.7 convert_element_type.103
  1.8 0.7 select_reduce_fusion.1
  2.5 0.0 copy-start
  2.6 1.0 copy-done
  3.6 1.0 copy-done.1
  4.6 100.7 %shard_map.110 = (bf16[16,128,2048]{2,1,0:T(8,128)(2,1)}, bf16[16,128,2048]{2,1,0:T(8,128)(2,1)}, bf16[16,16,128]{2,1,0:T(8,128)(2,1)S(1)}) custom-call(bf16[128,2048]{1,0:T(8,128)(2,1)S(1)} %copy-done, bf16[128,2048]{1,0:T(8,128)(2,1)S(1)} %copy-done.1, bf16[16,128]{1,0:T(8,128)(2,1)S(1)} %bitcast.58), custom_call_target="tpu_custom_call" | custom-call | tf_op jit(solution)/shard_map/pallas_call | solution.py:284
  105.4 0.6 dynamic-slice_convert_fusion
  106.0 0.3 reduce_window_sum.17
  106.3 4.9 %convolution_convert_fusion.2 = bf16[16,72,2048]{2,1,0:T(8,128)(2,1)S(1)} fusion(bf16[16,128,2048]{2,1,0:T(8,128)(2,1)} %get-tuple-element.13, s32[16,128]{1,0:T(8,128)S(1)} %broadcast_add_fusion, pred[16,128]{1,0:T(8,128)(4,1)S(1)} %get-tuple-element.22), kind=kOutput, calls=%fused_computation.10 | convolution fusion | flops 606633984 | bytes 13117440 | tf_op jit(solution)/shard_map/bst,btd->bsd/dot_general | solution.py:551
  111.2 0.9 copy-done.4
  112.1 1.4 convolution_convert_fusion.1
  113.5 0.0 copy-start.5
  113.5 0.2 slice-done.2
  113.7 0.6 slice-done.3
  114.3 2.4 fusion.20
  116.7 0.0 copy-done.5
  116.7 2.5 %multiply_convert_fusion.1 = (bf16[1152,384]{0,1:T(8,128)(2,1)S(1)}, f32[1152,384]{0,1:T(8,128)S(1)}) fusion(f32[1152,384]{0,1:T(8,128)S(1)} %fusion.20, bf16[1152,2048]{1,0:T(8,128)(2,1)S(1)} %bitcast.62, bf16[1,3,2048,384]{3,2,1,0:T(8,128)(2,1)S(1)} %bitcast.70), kind=kOutput, calls=%fused_computation.26 | convolution fusion | flops 1814593536 | bytes 10715136 | tf_op jit(solution)/shard_map/dot_general | solution.py:558
  119.2 0.0 copy-start.9
  119.2 0.0 copy-done.2
  119.2 3.6 %multiply_reduce_fusion = (bf16[1152]{0:T(1024)(128)(2,1)S(1)}, f32[1152,384]{0,1:T(8,128)}) fusion(bf16[1152,384]{0,1:T(8,128)(2,1)S(1)} %get-tuple-element.28, bf16[1152,2048]{1,0:T(8,128)(2,1)S(1)} %bitcast.59, bf16[1,3,2048,384]{3,2,1,0:T(8,128)(2,1)S(1)} %bitcast.70), kind=kOutput, calls=%fused_computation.25 | convolution fusion | flops 1813265280 | bytes 8947968 | tf_op jit(solution)/shard_map/dot_general | solution.py:562
  122.9 0.0 copy-done.9
  122.9 0.7 reshape.55
  123.6 1.8 fusion.42
  125.4 1.4 mul.118
  126.8 2.7 %multiply_convert_fusion.2 = (bf16[1152,384]{0,1:T(8,128)(2,1)S(1)}, bf16[1152,384]{0,1:T(8,128)(2,1)S(1)}) fusion(f32[1152,384]{0,1:T(8,128)} %get-tuple-element.31, f32[1152]{0:T(1024)} %mul.118, f32[1152,384]{0,1:T(8,128)S(1)} %fusion.20, f32[1152,384]{0,1:T(8,128)S(1)} %get-tuple-element.29), kind=kLoop, calls=%fused_computation.27 | loop fusion | flops 6193152 | bytes 7082496 | tf_op jit(solution)/shard_map/convert_element_type | solution.py:566
  129.5 0.2 copy-done.3
  129.7 1.8 multiply_convert_fusion
  131.5 0.0 copy-done.8
  131.5 0.1 select_convert_fusion.rt
  131.6 0.0 slice-done
  131.6 0.0 slice-done.1
  131.6 2.4 %fusion.31.g1 = bf16[1024,384]{1,0:T(8,128)(2,1)} fusion(bf16[1152,384]{0,1:T(8,128)(2,1)S(1)} %get-tuple-element.26, bf16[1152,2048]{1,0:T(8,128)(2,1)S(1)} %bitcast.65, s32[]{:T(128)S(6)} %select_n.28), kind=kOutput, calls=%fused_computation.42 | convolution fusion | flops 906362880 | bytes 4030468 | tf_op jit(solution)/shard_map/dot_general | solution.py:575
  134.0 1.5 fusion.28.g0
  135.6 2.4 %fusion.34.g2 = bf16[1024,384]{1,0:T(8,128)(2,1)} fusion(bf16[1152,384]{0,1:T(8,128)(2,1)S(1)} %copy-done.10, bf16[1152,2048]{1,0:T(8,128)(2,1)S(1)} %multiply_convert_fusion, s32[]{:T(128)S(6)} %select_n.28), kind=kOutput, calls=%fused_computation.43 | convolution fusion | flops 906362880 | bytes 4030468 | tf_op jit(solution)/shard_map/dot_general | solution.py:575
  138.0 2.7 %fusion.5.k2 = f32[1024,384]{1,0:T(8,128)} fusion(bf16[1152,384]{0,1:T(8,128)(2,1)S(1)} %copy-done.10, bf16[1152,2048]{1,0:T(8,128)(2,1)S(1)} %multiply_convert_fusion, s32[]{:T(128)S(6)} %select_n.29), kind=kOutput, calls=%fused_computation.13 | convolution fusion | flops 905969664 | bytes 4816900 | tf_op jit(solution)/shard_map/dot_general | solution.py:575
  140.7 2.7 %fusion.9.k1 = f32[1024,384]{1,0:T(8,128)} fusion(bf16[1152,384]{0,1:T(8,128)(2,1)S(1)} %get-tuple-element.26, bf16[1152,2048]{1,0:T(8,128)(2,1)S(1)} %bitcast.67, s32[]{:T(128)S(6)} %select_n.29), kind=kOutput, calls=%fused_computation.17 | convolution fusion | flops 905969664 | bytes 4816900 | tf_op jit(solution)/shard_map/dot_general | solution.py:575
  143.3 2.7 %fusion.11.k0 = f32[1024,384]{1,0:T(8,128)} fusion(bf16[1152,384]{0,1:T(8,128)(2,1)S(1)} %get-tuple-element.27, bf16[1152,2048]{1,0:T(8,128)(2,1)S(1)} %bitcast.68, s32[]{:T(128)S(6)} %select_n.29), kind=kOutput, calls=%fused_computation.19 | convolution fusion | flops 905969664 | bytes 4816900 | tf_op jit(solution)/shard_map/dot_general | solution.py:575
  146.0 0.0 slice-done.4
  146.0 2.9 %fusion.18 = f32[1152,2048]{1,0:T(8,128)S(1)} fusion(bf16[1152,384]{0,1:T(8,128)(2,1)S(1)} %get-tuple-element.27, bf16[1,3,2048,384]{3,2,1,0:T(8,128)(2,1)S(1)} %bitcast.72), kind=kOutput, calls=%fused_computation.31 | convolution fusion | flops 1811939328 | bytes 11894784 | tf_op jit(solution)/shard_map/dot_general | solution.py:581
  148.9 2.9 %fusion = bf16[1152,2048]{1,0:T(8,128)(2,1)S(1)} fusion(f32[1152,2048]{1,0:T(8,128)S(1)} %fusion.18, bf16[1152,384]{0,1:T(8,128)(2,1)S(1)} %get-tuple-element.26, bf16[1,3,2048,384]{3,2,1,0:T(8,128)(2,1)S(1)} %bitcast.72), kind=kOutput, calls=%fused_computation.2 | convolution fusion | flops 1816657920 | bytes 16613376 | tf_op jit(solution)/shard_map/dot_general | solution.py:582
  151.8 5.7 %convolution_convert_fusion.sp = bf16[16,128,2048]{2,1,0:T(8,128)(2,1)} fusion(bf16[16,72,2048]{2,1,0:T(8,128)(2,1)S(1)} %bitcast.60, s32[16,128]{1,0:T(8,128)S(1)} %broadcast_add_fusion, pred[16,128]{1,0:T(8,128)(4,1)S(1)} %get-tuple-element.22), kind=kOutput, calls=%fused_computation.4 | convolution fusion | flops 608468992 | bytes 13117440 | tf_op jit(solution)/shard_map/bst,bsd->btd/dot_general | solution.py:584
  157.5 72.6 %shard_map.111 = (bf16[128,2048]{1,0:T(8,128)(2,1)S(1)}, bf16[16,128]{1,0:T(8,128)(2,1)S(1)}, f32[3,1024,384]{2,1,0:T(8,128)}, f32[8,128]{1,0:T(8,128)S(1)}) custom-call(bf16[16,128,2048]{2,1,0:T(8,128)(2,1)} %convolution_convert_fusion.sp, bf16[16,16,128]{2,1,0:T(8,128)(2,1)S(1)} %select_convert_fusion.rt, bf16[1024,384]{1,0:T(8,128)(2,1)S(1)} %fusion.28.g0, ...), custom_call_target="tpu_custom_call" | custom-call | tf_op jit(solution)/shard_map/pallas_call | solution.py:503
  230.1 0.6 reduce_sum.59
  231.4 0.0 copy-done.7
  231.4 0.6 select_reduce_fusion
  232.0 7.7 %divide_convert_fusion = (bf16[1,3,1024,384]{3,2,1,0:T(8,128)(2,1)}, bf16[1,3,1024,384]{3,2,1,0:T(8,128)(2,1)}, bf16[1,3,1024,384]{3,2,1,0:T(8,128)(2,1)}) fusion(f32[3,1024,384]{2,1,0:T(8,128)} %get-tuple-element.18, bf16[1,3,1024,384]{3,2,1,0:T(8,128)(2,1)S(1)} %copy-done.6, bf16[1,3,1024,384]{3,2,1,0:T(8,128)(2,1)} %param.13, f32[]{:T(128)S(6)} %min.3), kind=kLoop, calls=%fused_computation.8 | loop fusion | flops 20054016 | bytes 16515076 | tf_op jit(solution)/shard_map/convert_element_type | solution.py:123
  239.7 0.8 copy.39
  (24 shorter events, 0.1 us)
Async XLA Ops:
  2.5 1.0 copy-start
  3.6 1.0 copy-start.1
  106.3 5.8 %copy-start.4 = (bf16[16,128,2048]{2,1,0:T(8,128)(2,1)S(1)}, bf16[16,128,2048]{2,1,0:T(8,128)(2,1)}, u32[]{:S(2)}) copy-start(bf16[16,128,2048]{2,1,0:T(8,128)(2,1)} %get-tuple-element.14) | copy-start | bytes 25165828
  106.3 7.4 %slice-start.2 = ((s8[4718592]{0:T(1024)(128)(4,1)}), s8[4194304]{0:T(1024)(128)(4,1)S(1)}, s32[]{:S(2)}) async-start(s8[4718592]{0:T(1024)(128)(4,1)} %bitcast.69), calls=%async_computation.2 | async-start | bytes 8388608
  112.1 7.1 %copy-start.2 = (bf16[16,72,2048]{2,1,0:T(8,128)(2,1)}, bf16[16,72,2048]{2,1,0:T(8,128)(2,1)S(1)}, u32[]{:S(2)}) copy-start(bf16[16,72,2048]{2,1,0:T(8,128)(2,1)S(1)} %convolution_convert_fusion.2) | copy-start | bytes 14155780
  112.1 2.2 slice-start.3
  113.5 3.2 %copy-start.5 = (bf16[16,72,2048]{2,1,0:T(8,128)(2,1)}, bf16[16,72,2048]{2,1,0:T(8,128)(2,1)S(1)}, u32[]{:S(2)}) copy-start(bf16[16,72,2048]{2,1,0:T(8,128)(2,1)S(1)} %convolution_convert_fusion.1) | copy-start | bytes 14155780
  119.2 3.6 %copy-start.9 = (bf16[1152,384]{0,1:T(8,128)(2,1)}, bf16[1152,384]{0,1:T(8,128)(2,1)S(1)}, u32[]{:S(2)}) copy-start(bf16[1152,384]{0,1:T(8,128)(2,1)S(1)} %get-tuple-element.28) | copy-start | bytes 2654212
  126.8 2.9 %copy-start.3 = (bf16[16,72,2048]{2,1,0:T(8,128)(2,1)S(1)}, bf16[16,72,2048]{2,1,0:T(8,128)(2,1)}, u32[]{:S(2)}) copy-start(bf16[16,72,2048]{2,1,0:T(8,128)(2,1)} %copy-done.2) | copy-start | bytes 14155780
  126.8 4.8 %slice-start = ((s8[4718592]{0:T(1024)(128)(4,1)}), s8[4194304]{0:T(1024)(128)(4,1)S(1)}, s32[]{:S(2)}) async-start(s8[4718592]{0:T(1024)(128)(4,1)} %bitcast.63), calls=%async_computation | async-start | bytes 8388608
  129.7 1.8 copy-start.8
  129.7 1.9 slice-start.1
  134.0 1.5 copy-start.10
  138.0 8.0 %slice-start.4 = ((s8[4718592]{0:T(1024)(128)(4,1)}), s8[524288]{0:T(1024)(128)(4,1)S(1)}, s32[]{:S(2)}) async-start(s8[4718592]{0:T(1024)(128)(4,1)} %bitcast.71), calls=%async_computation.4 | async-start | bytes 1048576
  140.6 5.3 %slice-start.5 = ((s8[4718592]{0:T(1024)(128)(4,1)}), s8[4194304]{0:T(1024)(128)(4,1)S(1)}, s32[]{:S(2)}) async-start(s8[4718592]{0:T(1024)(128)(4,1)} %bitcast.71), calls=%async_computation.5 | async-start | bytes 8388608
  157.5 73.9 %copy-start.7 = (s32[128,8]{0,1:T(8,128)S(1)}, s32[128,8]{0,1:T(8,128)}, u32[]{:S(2)}) copy-start(s32[128,8]{0,1:T(8,128)} %param.9) | copy-start | bytes 12292
  157.5 74.5 %copy-start.6 = (bf16[1,3,1024,384]{3,2,1,0:T(8,128)(2,1)S(1)}, bf16[1,3,1024,384]{3,2,1,0:T(8,128)(2,1)}, u32[]{:S(2)}) copy-start(bf16[1,3,1024,384]{3,2,1,0:T(8,128)(2,1)} %param.12) | copy-start | bytes 7077892
